TPU v7x, 256 devices: a whole 4x4x8 slice. The times are simulated.
256 devices in a mesh: seg: 8 (over z), tile: 32 (over x, y, core).
Axes of the slice: x: 4, y: 4, z: 8, core: 2. Of those that a mesh axis runs over, the one named last changes fastest.
Arguments:
- floc_attr: float32 [8, 4194304], P(None, ('seg', 'tile')), may hold values from -4 to 4, as said below
- floc_slot: int32 [4194304], P(('seg', 'tile')), may hold values from 0 to 32767, as said below
- same_pairs: int32 [8, 32, 2, 1024], P('seg', 'tile'), may hold values from 0 to 255, as said below
- same_count: int32 [8, 32], P('seg', 'tile'), may hold values from 128 to 1024, as said below
- adj_pairs: int32 [8, 32, 2, 128], P('seg', 'tile'), may hold values from 0 to 255, as said below
- neighbour_pair_count: int32 [8, 32], P('seg', 'tile'), may hold values from 32 to 128, as said below
Outputs:
- new_mass: float32 [4194304], P(('seg', 'tile'))
Inputs may be any that keep to these rules, and one draw needn't show every extreme that they name: `floc_slot`: on each owner the 16384 slots are distinct; in every segment one tile is sent 1024 flocs by every tile of the segment, which makes its buffer full. `same_pairs`: pairs of blocks of one cell owner; the partner lies within two blocks of the receiving block. `same_count`: some owner uses all 1024 entries. `adj_pairs`: A partner below 32 comes with an own block below 32; a partner of 32 or more with an own block of 224 or more. `neighbour_pair_count`: some owner uses all 128 entries. `floc_attr`: rows 0 to 5 are coordinates, row 6 masses, row 7 radii; masses and radii are positive.
All inputs are finite; a program needn't handle non-finite values.
Results may differ from a plain program's by a relative error of at most 0.0003.
Values sent between devices are 32-bit elements; how exact they have to be, the bound alone decides.
No kernel may reach another device: no remote copies, remote signals or barrier semaphores. Data moves between devices by JAX's collectives and lax.ppermute only.
A program may use at most 128 MiB of HBM per device.

v0:
```python
import jax
import jax.numpy as jnp
from jax import lax
from jax.sharding import PartitionSpec as P

ATTR = 8
BLOCK = 128
FLOC_DEV = 16384
NBLK = 256
EDGE = 32


WIDTH = 2.0
RATE = 0.05
GROUP = 16


def extended(cells, sides, width):
    for axis, dim in sides:
        count = lax.axis_size(axis)
        ends = count - 1
        head = lax.slice_in_dim(cells, 0, width, axis=dim)
        tail = lax.slice_in_dim(cells, cells.shape[dim] - width, cells.shape[dim], axis=dim)
        cells = jnp.concatenate(
            [
                lax.ppermute(tail, axis, [(i, (i + 1) % count) for i in range(ends)]),
                cells,
                lax.ppermute(head, axis, [((i + 1) % count, i) for i in range(ends)]),
            ],
            axis=dim,
        )
    return cells


def pairwise_gain_values(left, right, same_block):
    left_position = left[:, :6]
    right_position = right[:, :6]
    crossing_product = jnp.einsum(
        "rmh,rmw->rhw", left_position, right_position, precision=lax.Precision.HIGHEST
    )
    norm_l = jnp.sum(left_position * left_position, axis=1)
    norm_r = jnp.sum(right_position * right_position, axis=1)
    dist = norm_l[:, :, None] + norm_r[:, None, :] - 2.0 * crossing_product
    reach = left[:, 7][:, :, None] + right[:, 7][:, None, :]
    weight = reach * reach * jnp.exp(-dist / WIDTH)
    diag = jnp.arange(BLOCK)[:, None] == jnp.arange(BLOCK)[None, :]
    weight = jnp.where(same_block[:, None, None] & diag[None], 0.0, weight)
    return jnp.einsum("gpq,gq->gp", weight, right[:, 6], precision=lax.Precision.HIGHEST)


def sweep(table, first, second, count, gains):
    total = first.shape[0]

    def step(index, acc):
        low = index * GROUP
        owner_index_list = lax.dynamic_slice_in_dim(first, low, GROUP)
        other_ids = lax.dynamic_slice_in_dim(second, low, GROUP)
        left = jnp.take(table, owner_index_list, axis=0)
        right = jnp.take(table, other_ids, axis=0)
        part = pairwise_gain_values(left, right, owner_index_list == other_ids)
        live = low + jnp.arange(GROUP) < count
        part = jnp.where(live[:, None], part, 0.0)
        return acc.at[owner_index_list].add(part)

    upper = total // GROUP
    return lax.fori_loop(0, upper, step, gains)


def body(floc_attr, floc_slot, same_pairs, same_count, adj_pairs, neighbour_pair_count):
    tiles = lax.axis_size("tile")
    capacity = 2 * FLOC_DEV // tiles
    cap_blocks = capacity // BLOCK
    send = jnp.zeros((NBLK, ATTR, BLOCK), jnp.float32)
    send = send.at[floc_slot // BLOCK, :, floc_slot % BLOCK].set(floc_attr.T)
    send = send.reshape(tiles, cap_blocks, ATTR, BLOCK)
    owned = lax.all_to_all(send, "tile", split_axis=0, concat_axis=0, tiled=True).reshape(
        NBLK, ATTR, BLOCK
    )
    table = extended(owned, (("seg", 0),), EDGE)
    gains = jnp.zeros((NBLK + 2 * EDGE, BLOCK), jnp.float32)
    same_first = same_pairs[0, 0, 0] + EDGE
    same_second = same_pairs[0, 0, 1] + EDGE
    gains = sweep(table, same_first, same_second, same_count[0, 0], gains)
    adj_first = adj_pairs[0, 0, 0] + EDGE
    partner = adj_pairs[0, 0, 1]
    adj_second = jnp.where(partner < EDGE, partner, partner + NBLK)
    gains = sweep(table, adj_first, adj_second, neighbour_pair_count[0, 0], gains)
    owned_gain = gains[EDGE : EDGE + NBLK].reshape(tiles, cap_blocks, BLOCK)
    returned = lax.all_to_all(owned_gain, "tile", split_axis=0, concat_axis=0, tiled=True).reshape(
        NBLK * BLOCK
    )
    selected_pairs = jnp.take(returned, floc_slot, axis=0)
    return floc_attr[6] + RATE * selected_pairs


def solution(mesh):
    placed = (
        P(None, ("seg", "tile")),
        P(("seg", "tile")),
        P("seg", "tile", None, None),
        P("seg", "tile"),
        P("seg", "tile", None, None),
        P("seg", "tile"),
    )
    return jax.shard_map(
        body, mesh=mesh, in_specs=placed, out_specs=P(("seg", "tile")), check_vma=False
    )
```

profile of v0, /device:TPU:97, one launch (start us, length us, event | category | flops | bytes accessed | tf_op | source)
XLA Modules:
  0.0 719.3 jit_solution(18429845045516671900)
XLA Ops:
  2.8 5.7 copy.9
  8.5 47.4 %scatter_custom_fusion.2 = f32[32768,8]{1,0:T(8,128)} fusion(s32[16384]{0:T(1024)S(1)} %broadcast_select_fusion.4, f32[16384,8]{1,0:T(8,128)} %copy.9, f32[]{:T(128)} %constant.159.clone.1), kind=kCustom, calls=%fused_computation.64 | custom fusion | bytes 1049088
  55.9 9.8 %copy.10 = f32[32,8,8,128]{3,2,1,0:T(8,128)} copy(f32[32,8,8,128]{2,3,1,0:T(8,128)} %bitcast.66) | data formatting | bytes 2097152 | tf_op jit(solution)/shard_map/reshape | solution.py:75
  65.7 7.8 %all-to-all-start = ((f32[32,8,8,128]{3,2,1,0:T(8,128)}), f32[32,8,8,128]{3,2,1,0:T(8,128)S(1)}, u32[]{:S(2)}, u32[]{:S(2)}) async-start(f32[32,8,8,128]{3,2,1,0:T(8,128)} %copy.10), calls=%async_computation | async-start | bytes 2097152 | tf_op jit(solution)/shard_map/all_to_all | solution.py:76
  73.5 16.9 %all-to-all-done = f32[32,8,8,128]{3,2,1,0:T(8,128)S(1)} async-done(((f32[32,8,8,128]{3,2,1,0:T(8,128)}), f32[32,8,8,128]{3,2,1,0:T(8,128)S(1)}, u32[]{:S(2)}, u32[]{:S(2)}) %all-to-all-start) | async-done | bytes 1048608 | tf_op jit(solution)/shard_map/all_to_all | solution.py:76
  90.4 4.8 collective-permute-start
  97.9 5.0 collective-permute-done.1
  103.0 455.0 %while.26 = (s32[]{:T(128)}, f32[320,128]{1,0:T(8,128)S(1)}, s32[1024]{0:T(1024)S(1)}, s32[]{:T(128)}, s32[1024]{0:T(1024)S(1)}, /*index=5*/f32[320,8,128]{2,1,0...) while((s32[]{:T(128)}, f32[320,128]{1,0:T(8,128)S(1)}, s32[1024]{0:T(1024)S(1)}, ...), condition=%wide.region_5.7_spmd, body=%wide.region_1.6_spmd.sunk | while | flops 24742132 | bytes 3163419 | solution.py:66
  104.6 2.3 fusion.50
  118.8 2.3 fusion.50
  147.3 2.3 fusion.50
  154.4 2.3 fusion.50
  182.8 2.3 fusion.50
  197.0 2.3 fusion.50
  204.1 2.3 fusion.50
  232.6 2.3 fusion.50
  239.7 2.3 fusion.50
  268.1 2.3 fusion.50
  282.3 2.3 fusion.50
  289.4 2.3 fusion.50
  310.8 2.3 fusion.50
  317.9 2.3 fusion.50
  332.1 2.3 fusion.50
  353.4 2.3 fusion.50
  367.6 2.3 fusion.50
  396.1 2.3 fusion.50
  403.2 2.3 fusion.50
  431.6 2.3 fusion.50
  558.0 56.9 %while.27 = (s32[]{:T(128)}, f32[320,128]{1,0:T(8,128)S(1)}, s32[128]{0:T(128)S(1)}, s32[]{:T(128)}, s32[128]{0:T(128)S(1)}, /*index=5*/f32[320,8,128]{2,1,0:T(8...) while((s32[]{:T(128)}, f32[320,128]{1,0:T(8,128)S(1)}, s32[128]{0:T(128)S(1)}, ...), condition=%wide.region_10.12_spmd, body=%wide.region_6.11_spmd.sunk | while | flops 24742132 | bytes 3163419 | solution.py:66
  615.5 4.8 all-to-all-start.1
  621.4 6.7 all-to-all-done.1
  628.1 90.5 %gather_fusion.4 = f32[16384]{0:T(1024)S(1)} fusion(f32[32768]{0:T(1024)S(1)} %bitcast.65, s32[16384]{0:T(1024)S(1)} %get-tuple-element.268), kind=kCustom, calls=%fused_computation.4 | custom fusion | bytes 196608 | tf_op jit(solution)/shard_map/jit(_take)/gather | solution.py:92
  (1153 shorter events, 464.9 us)
Async XLA Ops:
  55.9 17.6 %copy-start.2 = (s32[1,1,2,128]{3,2,1,0:T(2,128)S(1)}, s32[1,1,2,128]{3,2,1,0:T(2,128)}, u32[]{:S(2)}) copy-start(s32[1,1,2,128]{3,2,1,0:T(2,128)} %param.16) | copy-start | bytes 3076
  55.9 17.6 %copy-start.1 = (s32[1,1,2,1024]{3,2,1,0:T(2,128)S(1)}, s32[1,1,2,1024]{3,2,1,0:T(2,128)}, u32[]{:S(2)}) copy-start(s32[1,1,2,1024]{3,2,1,0:T(2,128)} %param.14) | copy-start | bytes 24580
  65.7 24.7 %all-to-all-start = ((f32[32,8,8,128]{3,2,1,0:T(8,128)}), f32[32,8,8,128]{3,2,1,0:T(8,128)S(1)}, u32[]{:S(2)}, u32[]{:S(2)}) async-start(f32[32,8,8,128]{3,2,1,0:T(8,128)} %copy.10), calls=%async_computation | async-start | bytes 2097152 | tf_op jit(solution)/shard_map/all_to_all | solution.py:76
  90.4 7.5 %collective-permute-start = (f32[32,8,128]{2,1,0:T(8,128)S(1)}, f32[32,8,128]{2,1,0:T(8,128)S(1)}, u32[]{:S(2)}, u32[]{:S(2)}) collective-permute-start(f32[32,8,128]{2,1,0:T(8,128)S(1)} %bitcast.81), channel_id=1, source_target_pairs={{0,32},{32,64},{64,96},{96,128},{128,160},{160,192},{192,224},{1,3... | collective-permute-start | bytes 393224 | tf_op jit(solution)/shard_map/ppermute | solution.py:26
  95.2 7.7 %collective-permute-start.1 = (f32[32,8,128]{2,1,0:T(8,128)S(1)}, f32[32,8,128]{2,1,0:T(8,128)S(1)}, u32[]{:S(2)}, u32[]{:S(2)}) collective-permute-start(f32[32,8,128]{2,1,0:T(8,128)S(1)} %bitcast.80), channel_id=1, source_target_pairs={{32,0},{64,32},{96,64},{128,96},{160,128},{192,160},{224,192},{33,... | collective-permute-start | bytes 393224 | tf_op jit(solution)/shard_map/ppermute | solution.py:28
  615.5 12.6 %all-to-all-start.1 = ((f32[32,8,128]{2,1,0:T(8,128)}), f32[32,8,128]{2,1,0:T(8,128)S(1)}, u32[]{:S(2)}, u32[]{:S(2)}) async-start(f32[32,8,128]{2,1,0:T(8,128)} %slice_bitcast_fusion.4), calls=%async_computation.1 | async-start | bytes 262144 | tf_op jit(solution)/shard_map/all_to_all | solution.py:89
  628.1 90.5 %copy-start = (s32[16384]{0:T(1024)S(1)}, s32[16384]{0:T(1024)}, u32[]{:S(2)}) copy-start(s32[16384]{0:T(1024)} %param.13) | copy-start | bytes 196612
where the time goes:
time: 722 us; the launch traced here: 719 us
  matrix products  290 us (40%)
  local copies, waits for them, and re-layouts  238 us (33%)
  other arithmetic  134 us (19%)
  waiting for transfers between devices  29.2 us (4%)
  starting transfers between devices  19.4 us (3%)
  loops' own time  8.75 us (1%)
    dot_general x72, matrix products, pairwise_gain_values(): jnp.einsum('rmh,rmw->rhw', left_position, right_position, precision=lax.P...  166 us
    dot_general x72, matrix products, pairwise_gain_values(): jnp.einsum('gpq,gq->gp', weight, right[:, 6], precision=lax.Precision.HIG...  124 us
    gather x1, local copies, waits for them, and re-layouts, body(): selected_pairs = jnp.take(returned, floc_slot, axis=0)  90.5 us
    scatter-add x72, other arithmetic, step(): return acc.at[owner_index_list].add(part)  58.3 us
    lt x72, other arithmetic, step(): live = low + jnp.arange(GROUP) < count  48.1 us
    unnamed x7, local copies, waits for them, and re-layouts  47.4 us
    gather x72, local copies, waits for them, and re-layouts, step(): left = jnp.take(table, owner_index_list, axis=0)  40.7 us
    gather x72, local copies, waits for them, and re-layouts, step(): right = jnp.take(table, other_ids, axis=0)  40.7 us
  transfers between devices with their start and end apart: 4, of which 4 were waited for; matrix products, arithmetic and copies ran while one was open for 0% of the time, Pallas kernels for 0%

commit v1 on v0

v1 whole, which is shorter than its diff:
```python
import functools

import jax
import jax.numpy as jnp
import numpy as np
from jax import lax
from jax.experimental import pallas as pl
from jax.experimental.pallas import tpu as pltpu
from jax.sharding import PartitionSpec as P

ATTR = 8
BLOCK = 128
FLOC_DEV = 16384
NBLK = 256
EDGE = 32
RATE = 0.05
PSAME = 1024
PADJ = 128
SCALE = float(np.sqrt(np.log2(np.e)))
CHUNK = 1024
GCHUNK = 1024
KF = 48
SAME_UNROLL = 8
ADJ_UNROLL = 8
QROWS = 32
MIB = 2**20
BF = jnp.bfloat16
F32 = jnp.float32


def rounded(x):
    return x.astype(BF).astype(F32)


def onehot_rows(rows, index):
    shape = (rows, index.shape[1])
    return jnp.where(lax.broadcasted_iota(jnp.int32, shape, 0) == index, 1.0, 0.0)


def scatter_kernel(attr_ref, slot_ref, pairs_ref, count_ref, out_ref, mult_ref, y_ref, b_ref, acc_ref):
    first = pairs_ref[0:1, :]
    offset = pairs_ref[1:2, :] - first + 2
    live = lax.broadcasted_iota(jnp.int32, (1, PSAME), 1) < count_ref[0, 0]
    offset = jnp.where(live, offset, -1)
    mult_ref[...] = lax.dot_general(
        onehot_rows(8, offset).astype(BF),
        onehot_rows(NBLK, first).astype(BF),
        (((1,), (1,)), ((), ())),
        preferred_element_type=F32,
    )
    row = lax.broadcasted_iota(jnp.int32, (ATTR, CHUNK), 0)

    def step(s, carry):
        low = pl.multiple_of(s * CHUNK, CHUNK)
        slot = slot_ref[:, pl.ds(low, CHUNK)]
        block = onehot_rows(NBLK, slot >> 7).astype(BF)
        b_ref[:, :CHUNK] = block
        b_ref[:, CHUNK:] = block
        lane = lax.broadcasted_iota(jnp.int32, (BLOCK, CHUNK), 0) == (slot & 127)
        value = attr_ref[:, pl.ds(low, CHUNK)]
        value = jnp.where(row < 6, value * SCALE, value)
        high = rounded(value)
        rest = value - high
        for a in range(ATTR):
            at = slice(a * BLOCK, (a + 1) * BLOCK)
            y_ref[at, :CHUNK] = jnp.where(lane, high[a : a + 1], 0.0).astype(BF)
            y_ref[at, CHUNK:] = jnp.where(lane, rest[a : a + 1], 0.0).astype(BF)
        acc_ref[...] += lax.dot_general(
            y_ref[...], b_ref[...], (((1,), (1,)), ((), ())), preferred_element_type=F32
        )
        return carry

    acc_ref[...] = jnp.zeros_like(acc_ref)
    lax.fori_loop(0, FLOC_DEV // CHUNK, step, 0)
    for a in range(ATTR):
        out_ref[:, a, :] = acc_ref[a * BLOCK : (a + 1) * BLOCK, :].T


def forms(v):
    row = lax.broadcasted_iota(jnp.int32, (8, BLOCK), 0)
    six = row < 6
    lo3 = row < 3
    high = rounded(v)
    rest = v - high
    norm = -0.5 * jnp.sum(jnp.where(six, v * v, 0.0), axis=0, keepdims=True)
    radius = v[7:8]
    x = jnp.where(lo3, jnp.broadcast_to(norm, (8, BLOCK)), jnp.broadcast_to(radius * radius, (8, BLOCK)))
    p0 = rounded(x)
    p1 = rounded(x - p0)
    p2 = x - p0 - p1
    k = jnp.where(lo3, row, row - 3)
    own = jnp.where(six, jnp.where(k == 0, p0, jnp.where(k == 1, p1, p2)), 0.0)
    one = jnp.ones((8, BLOCK), F32)
    zero = jnp.zeros((8, BLOCK), F32)
    mid3 = (row >= 3) & six
    left = jnp.concatenate([high, high, rest, rest, own, jnp.where(six, one, zero)], axis=0)
    h6 = jnp.where(six, high, 0.0)
    m6 = jnp.where(six, rest, 0.0)
    h7 = jnp.where(row == 7, 2.0 * high, 0.0)
    m7 = jnp.where(row == 7, 2.0 * rest, 0.0)
    arg = [h6, m6, h6, m6, jnp.where(lo3, one, zero), jnp.where(lo3, own, 0.0)]
    reach = [h7, m7, h7, m7, jnp.where(mid3, one, zero), jnp.where(mid3, own, 0.0)]
    right = jnp.concatenate([jnp.concatenate(arg, axis=0), jnp.concatenate(reach, axis=0)], axis=1)
    return left, right


def partner_form(v, left, j, xt_ref, mb_ref):
    turned = jnp.concatenate([left, v], axis=0).T
    xt_ref[j] = turned[:, :KF].astype(BF)
    mb_ref[j] = jnp.broadcast_to(turned[:, KF + 6 : KF + 7], (BLOCK, BLOCK))


def same_kernel(o_ref, mult_ref, out_ref, xt_ref, r_ref, mb_ref):
    zero_right = jnp.zeros((KF, 2 * BLOCK), BF)
    r_ref[0] = zero_right
    r_ref[1] = zero_right

    def build(j, carry):
        v = o_ref[j]
        left, right = forms(v)
        r_ref[j + 2] = right.astype(BF)
        partner_form(v, left, j, xt_ref, mb_ref)
        return carry

    lax.fori_loop(0, NBLK, build, 0, unroll=4)
    lane = lax.broadcasted_iota(jnp.int32, (QROWS, BLOCK), 1)
    sub = lax.broadcasted_iota(jnp.int32, (QROWS, BLOCK), 0)

    def main(j, carry):
        f1, f2 = carry
        j1 = jnp.maximum(j - 1, 0)
        j2 = jnp.maximum(j - 2, 0)
        rhs = jnp.concatenate([r_ref[j + 2], r_ref[j + 1], r_ref[j]], axis=1)
        mass1 = o_ref[j1][6:7] * mult_ref[1, j]
        mass2 = o_ref[j2][6:7] * mult_ref[0, j]
        acc = [jnp.zeros((8, BLOCK), F32) for _ in range(3)]
        rev = []
        for q in range(BLOCK // QROWS):
            at = slice(q * QROWS, (q + 1) * QROWS)
            d = jnp.dot(xt_ref[j, at, :], rhs, preferred_element_type=F32)
            mb = mb_ref[j, at, :]
            w = []
            for a in range(3):
                low = a * 2 * BLOCK
                e = jnp.exp2(d[:, low : low + BLOCK]) * d[:, low + BLOCK : low + 2 * BLOCK]
                if a == 0:
                    e = jnp.where(lane == sub + q * QROWS, 0.0, e)
                w.append(e)
                acc[a] = acc[a] + jnp.sum((e * mb).reshape(QROWS // 8, 8, BLOCK), axis=0)
            rev.append(w[1] * mass1 + w[2] * mass2)
        back = jnp.sum(jnp.concatenate(rev, axis=0).T.reshape(BLOCK // 8, 8, BLOCK), axis=0)
        f0 = acc[0] * mult_ref[2, j] + back
        f1 = f1 + acc[1] * mult_ref[3, j1]
        f2 = f2 + acc[2] * mult_ref[4, j2]
        out_ref[pl.ds(j2, 1), :] = jnp.sum(f2, axis=0, keepdims=True)
        return f0, f1

    zero = jnp.zeros((8, BLOCK), F32)
    f0, f1 = lax.fori_loop(0, NBLK, main, (zero, zero), unroll=SAME_UNROLL)
    out_ref[NBLK - 1 : NBLK, :] = jnp.sum(f0, axis=0, keepdims=True)
    out_ref[NBLK - 2 : NBLK - 1, :] = jnp.sum(f1, axis=0, keepdims=True)


def adj_kernel(o_ref, up_ref, down_ref, gain_ref, pairs_ref, count_ref, out_ref, xt_ref, r_ref, mb_ref):
    out_ref[...] = gain_ref[...]

    def build(j, carry):
        for half, ref in ((0, up_ref), (1, down_ref)):
            v = ref[j]
            left, _ = forms(v)
            partner_form(v, left, j + half * EDGE, xt_ref, mb_ref)
            _, right = forms(o_ref[j + half * (NBLK - EDGE)])
            r_ref[j + half * EDGE] = right.astype(BF)
        return carry

    lax.fori_loop(0, EDGE, build, 0, unroll=2)
    count = count_ref[0, 0]

    def main(u, carry):
        found = []
        for x in range(ADJ_UNROLL):
            t = u * ADJ_UNROLL + x
            i = jnp.clip(pairs_ref[0, t], 0, NBLK - 1)
            j = jnp.clip(pairs_ref[1, t], 0, 2 * EDGE - 1)
            k = jnp.clip(jnp.where(i < EDGE, i, i - (NBLK - 2 * EDGE)), 0, 2 * EDGE - 1)
            d = jnp.dot(xt_ref[j], r_ref[k], preferred_element_type=F32)
            e = jnp.exp2(d[:, :BLOCK]) * d[:, BLOCK:] * mb_ref[j]
            found.append((i, jnp.where(t < count, jnp.sum(e, axis=0, keepdims=True), 0.0)))
        for i, e in found:
            out_ref[pl.ds(i, 1), :] += e
        return carry

    lax.fori_loop(0, (count + ADJ_UNROLL - 1) // ADJ_UNROLL, main, 0)


def gather_kernel(gain_ref, slot_ref, attr_ref, out_ref):
    turned = gain_ref[...].T
    high = rounded(turned)
    table = jnp.concatenate([high, turned - high], axis=1).astype(BF)

    def step(s, carry):
        low = pl.multiple_of(s * GCHUNK, GCHUNK)
        slot = slot_ref[:, pl.ds(low, GCHUNK)]
        block = onehot_rows(NBLK, slot >> 7).astype(BF)
        z = jnp.dot(table, jnp.concatenate([block, block], axis=0), preferred_element_type=F32)
        lane = lax.broadcasted_iota(jnp.int32, (BLOCK, GCHUNK), 0) == (slot & 127)
        gain = jnp.sum(jnp.where(lane, z, 0.0), axis=0, keepdims=True)
        out_ref[:, pl.ds(low, GCHUNK)] = attr_ref[6:7, pl.ds(low, GCHUNK)] + RATE * gain
        return carry

    lax.fori_loop(0, FLOC_DEV // GCHUNK, step, 0)


VMEM = pl.BlockSpec(memory_space=pltpu.VMEM)
SMEM = pl.BlockSpec(memory_space=pltpu.SMEM)


def call(kernel, name, out, ins, scratch, cost, *args):
    return pl.pallas_call(
        kernel,
        out_shape=out,
        in_specs=ins,
        out_specs=jax.tree.map(lambda _: VMEM, out),
        scratch_shapes=scratch,
        compiler_params=pltpu.CompilerParams(vmem_limit_bytes=52 * MIB),
        cost_estimate=pl.CostEstimate(flops=cost, bytes_accessed=2 * MIB, transcendentals=0),
        name=name,
    )(*args)


def shape(*dims):
    return jax.ShapeDtypeStruct(dims, F32)


def body(floc_attr, floc_slot, same_pairs, same_count, adj_pairs, neighbour_pair_count):
    tiles = lax.axis_size("tile")
    cap_blocks = NBLK // tiles
    segs = lax.axis_size("seg")
    slot_row = floc_slot.reshape(1, FLOC_DEV)
    send, mult = call(
        scatter_kernel,
        "scatter",
        (shape(NBLK, ATTR, BLOCK), shape(8, NBLK)),
        [VMEM, VMEM, VMEM, SMEM],
        [
            pltpu.VMEM((ATTR * BLOCK, 2 * CHUNK), BF),
            pltpu.VMEM((NBLK, 2 * CHUNK), BF),
            pltpu.VMEM((ATTR * BLOCK, NBLK), F32),
        ],
        2 * 2 * ATTR * BLOCK * NBLK * FLOC_DEV,
        floc_attr,
        slot_row,
        same_pairs.reshape(2, PSAME),
        same_count,
    )
    send = send.reshape(tiles, cap_blocks, ATTR, BLOCK)
    owned = lax.all_to_all(send, "tile", split_axis=0, concat_axis=0, tiled=True)
    owned = owned.reshape(NBLK, ATTR, BLOCK)
    up = lax.ppermute(owned[NBLK - EDGE :], "seg", [(i, i + 1) for i in range(segs - 1)])
    down = lax.ppermute(owned[:EDGE], "seg", [(i + 1, i) for i in range(segs - 1)])
    gain = call(
        same_kernel,
        "same_pairs",
        shape(NBLK, BLOCK),
        [VMEM, SMEM],
        [
            pltpu.VMEM((NBLK, BLOCK, KF), BF),
            pltpu.VMEM((NBLK + 2, KF, 2 * BLOCK), BF),
            pltpu.VMEM((NBLK, BLOCK, BLOCK), F32),
        ],
        40_000_000_000,
        owned,
        mult,
    )
    gain = call(
        adj_kernel,
        "adjacent_pairs",
        shape(NBLK, BLOCK),
        [VMEM, VMEM, VMEM, VMEM, SMEM, SMEM],
        [
            pltpu.VMEM((2 * EDGE, BLOCK, KF), BF),
            pltpu.VMEM((2 * EDGE, KF, 2 * BLOCK), BF),
            pltpu.VMEM((2 * EDGE, BLOCK, BLOCK), F32),
        ],
        10_000_000_000,
        owned,
        up,
        down,
        gain,
        adj_pairs.reshape(2, PADJ),
        neighbour_pair_count,
    )
    gain = gain.reshape(tiles, cap_blocks, BLOCK)
    returned = lax.all_to_all(gain, "tile", split_axis=0, concat_axis=0, tiled=True)
    out = call(
        gather_kernel,
        "final_gather",
        shape(1, FLOC_DEV),
        [VMEM, VMEM, VMEM],
        [],
        10_000_000_000,
        returned.reshape(NBLK, BLOCK),
        slot_row,
        floc_attr,
    )
    return out.reshape(FLOC_DEV)


def solution(mesh):
    placed = (
        P(None, ("seg", "tile")),
        P(("seg", "tile")),
        P("seg", "tile", None, None),
        P("seg", "tile"),
        P("seg", "tile", None, None),
        P("seg", "tile"),
    )
    return jax.shard_map(
        body, mesh=mesh, in_specs=placed, out_specs=P(("seg", "tile")), check_vma=False
    )
```

time: 722 us -> 125 us (0.17)
  matrix products: 290 us -> 0 us
  local copies, waits for them, and re-layouts: 238 us -> 3.26 us
  other arithmetic: 134 us -> 0 us
  Pallas kernels: 0 us -> 77 us
  waiting for transfers between devices: 29.2 us -> 16.3 us
  blocking collectives: 0 us -> 11.9 us
  loops' own time: 8.75 us -> 0 us
    dot_general x144 -> x0, matrix products: 290 us -> none  [the longest x72 166 us: pairwise_gain_values(): jnp.einsum('rmh,rmw->rhw', left_position, right_position, precision=lax.P...]
    gather x145 -> x0, local copies, waits for them, and re-layouts: 172 us -> none  [the longest x1 90.5 us: body(): selected_pairs = jnp.take(returned, floc_slot, axis=0)]
    pallas_call x0 -> x4, Pallas kernels: none -> 77 us  [call(): pl.pallas_call(kernel, out_shape=out, in_specs=ins, out_specs=jax.tree.ma...]
    scatter-add x72 -> x0, other arithmetic: 58.3 us -> none  [step(): return acc.at[owner_index_list].add(part)]
    lt x72 -> x0, other arithmetic: 48.1 us -> none  [step(): live = low + jnp.arange(GROUP) < count]
    unnamed x7 -> x12, local copies, waits for them, and re-layouts: 47.4 us -> 3.24 us
    select_n x145 -> x0, other arithmetic: 12 us -> none  [the longest x72 5.99 us: step(): left = jnp.take(table, owner_index_list, axis=0)]
    all_to_all x0 -> x1, blocking collectives: none -> 11.9 us  [body(): lax.all_to_all(gain, 'tile', split_axis=0, concat_axis=0, tiled=True)]
  transfers between devices with their start and end apart: 4 -> 3, of which waited for: 4 -> 1; matrix products, arithmetic and copies ran while one was open for 0% -> 0% of each run, Pallas kernels for 0% -> 30%
where the time goes in v1:
time: 125 us; the launch traced here: 124 us
  Pallas kernels  77 us (62%)
  waiting for transfers between devices  16.3 us (13%)
  starting transfers between devices  14.4 us (12%)
  blocking collectives  11.9 us (10%)
  local copies, waits for them, and re-layouts  3.26 us (3%)
  between operations  1.38 us (1%)
    pallas_call x4, Pallas kernels, call(): pl.pallas_call(kernel, out_shape=out, in_specs=ins, out_specs=jax.tree.ma...  77 us
    all_to_all x1, waiting for transfers between devices, body(): lax.all_to_all(send, 'tile', split_axis=0, concat_axis=0, tiled=True)  16.3 us
    all_to_all x1, blocking collectives, body(): lax.all_to_all(gain, 'tile', split_axis=0, concat_axis=0, tiled=True)  11.9 us
    all_to_all x1, starting transfers between devices, body(): lax.all_to_all(send, 'tile', split_axis=0, concat_axis=0, tiled=True)  7.71 us
    ppermute x1, starting transfers between devices, body(): lax.ppermute(owned[NBLK - EDGE:], 'seg', [(i, i + 1) for i in range(segs...  4.75 us
    unnamed x12, local copies, waits for them, and re-layouts  3.24 us
  transfers between devices with their start and end apart: 3, of which 1 were waited for; matrix products, arithmetic and copies ran while one was open for 0% of the time, Pallas kernels for 30%

profile of v1, /device:TPU:97, one launch (start us, length us, event | category | flops | bytes accessed | tf_op | source)
XLA Modules:
  0.0 124.2 jit_solution(11610134289263604726)
XLA Ops:
  0.7 0.0 copy-start
  0.7 1.0 copy-done
  1.7 0.0 copy-start.2
  1.7 0.8 copy-done.2
  2.5 0.0 copy-start.4
  2.5 0.7 copy-done.4
  3.2 22.5 %scatter.1 = (f32[256,8,128]{2,1,0:T(8,128)}, f32[8,256]{1,0:T(8,128)S(1)}) custom-call(f32[8,16384]{1,0:T(8,128)S(1)} %copy-done, s32[1,16384]{1,0:T(1,128)S(1)} %bitcast.14, s32[2,1024]{1,0:T(2,128)S(1)} %bitcast.16, s32[1,1]{1,0:T(1,128)S(6)} %copy.7.count_ref), custom_call_target="tpu_custom_call" | custom-call | flops 17179869184 | bytes 2097152 | tf_op jit(solution)/shard_map/scatter/pallas_call | solution.py:219
  25.7 7.7 %all-to-all-start = ((f32[32,8,8,128]{3,2,1,0:T(8,128)}), f32[32,8,8,128]{3,2,1,0:T(8,128)S(1)}, u32[]{:S(2)}, u32[]{:S(2)}) async-start(f32[32,8,8,128]{3,2,1,0:T(8,128)} %bitcast.2), calls=%async_computation | async-start | bytes 2097152 | tf_op jit(solution)/shard_map/all_to_all | solution.py:257
  34.1 16.3 %all-to-all-done = f32[32,8,8,128]{3,2,1,0:T(8,128)S(1)} async-done(((f32[32,8,8,128]{3,2,1,0:T(8,128)}), f32[32,8,8,128]{3,2,1,0:T(8,128)S(1)}, u32[]{:S(2)}, u32[]{:S(2)}) %all-to-all-start) | async-done | bytes 1048608 | tf_op jit(solution)/shard_map/all_to_all | solution.py:257
  50.4 4.8 %collective-permute-start = (f32[32,8,128]{2,1,0:T(8,128)S(1)}, f32[32,8,128]{2,1,0:T(8,128)S(1)}, u32[]{:S(2)}, u32[]{:S(2)}) collective-permute-start(f32[32,8,128]{2,1,0:T(8,128)S(1)} %bitcast.19), channel_id=1, source_target_pairs={{0,32},{32,64},{64,96},{96,128},{128,160},{160,192},{192,224},{1,3... | collective-permute-start | bytes 393224 | tf_op jit(solution)/shard_map/ppermute | solution.py:259
  55.1 1.9 %collective-permute-start.1 = (f32[32,8,128]{2,1,0:T(8,128)S(1)}, f32[32,8,128]{2,1,0:T(8,128)S(1)}, u32[]{:S(2)}, u32[]{:S(2)}) collective-permute-start(f32[32,8,128]{2,1,0:T(8,128)S(1)} %bitcast.18), channel_id=1, source_target_pairs={{32,0},{64,32},{96,64},{128,96},{160,128},{192,160},{224,192},{33,... | collective-permute-start | bytes 393224 | tf_op jit(solution)/shard_map/ppermute | solution.py:260
  57.1 37.7 %same_pairs.1.gain_ref = f32[256,128]{1,0:T(8,128)S(1)} custom-call(f32[256,8,128]{2,1,0:T(8,128)S(1)} %bitcast.10, f32[8,256]{1,0:T(8,128)S(1)} %get-tuple-element.8.mult_ref), custom_call_target="tpu_custom_call" | custom-call | flops 40000000000 | bytes 2097152 | tf_op jit(solution)/shard_map/same_pairs/pallas_call | solution.py:219
  94.8 0.0 copy-start.5
  94.8 0.0 collective-permute-done.up_ref
  94.8 0.0 collective-permute-done.1.down_ref
  94.8 0.7 copy-done.5
  95.5 0.0 copy-start.1
  95.5 9.5 %adjacent_pairs.1 = f32[256,128]{1,0:T(8,128)S(1)} custom-call(f32[256,8,128]{2,1,0:T(8,128)S(1)} %bitcast.11, f32[32,8,128]{2,1,0:T(8,128)S(1)} %collective-permute-done.up_ref, f32[32,8,128]{2,1,0:T(8,128)S(1)} %collective-permute-done.1.down_ref, f32[256,128]{1,0:T(8,128)S(1)} %same_pairs.1.gain_ref, s32[2,128]{1,0:T(2,128)S(1)} %bitcast.17, ...), custom_call_target="tpu_custom_call" | custom-call | flops 10000000000 | bytes 2097152 | tf_op jit(solution)/shard_map/adjacent_pairs/pallas_call | solution.py:219
  105.0 0.0 copy-start.3
  105.0 11.9 %all_to_all.10 = f32[32,8,128]{2,1,0:T(8,128)S(1)} all-to-all(f32[32,8,128]{2,1,0:T(8,128)S(1)} %bitcast.12), channel_id=1, replica_groups=mesh['seg'=8,'tile'=32] {'tile'}, dimensions={0} | all-to-all | bytes 262144 | tf_op jit(solution)/shard_map/all_to_all | solution.py:294
  116.9 0.0 copy-done.1
  116.9 0.0 copy-done.3
  116.9 7.3 %final_gather.1 = f32[1,16384]{1,0:T(1,128)} custom-call(f32[256,128]{1,0:T(8,128)S(1)} %bitcast.13, s32[1,16384]{1,0:T(1,128)S(1)} %bitcast.15, f32[8,16384]{1,0:T(8,128)S(1)} %copy-done.1), custom_call_target="tpu_custom_call" | custom-call | flops 10000000000 | bytes 2097152 | tf_op jit(solution)/shard_map/final_gather/pallas_call | solution.py:219
  (1 shorter events, 0.0 us)
Async XLA Ops:
  0.7 1.0 copy-start
  1.7 0.8 copy-start.2
  2.5 0.7 copy-start.4
  25.7 24.6 %all-to-all-start = ((f32[32,8,8,128]{3,2,1,0:T(8,128)}), f32[32,8,8,128]{3,2,1,0:T(8,128)S(1)}, u32[]{:S(2)}, u32[]{:S(2)}) async-start(f32[32,8,8,128]{3,2,1,0:T(8,128)} %bitcast.2), calls=%async_computation | async-start | bytes 2097152 | tf_op jit(solution)/shard_map/all_to_all | solution.py:257
  50.4 44.4 %collective-permute-start = (f32[32,8,128]{2,1,0:T(8,128)S(1)}, f32[32,8,128]{2,1,0:T(8,128)S(1)}, u32[]{:S(2)}, u32[]{:S(2)}) collective-permute-start(f32[32,8,128]{2,1,0:T(8,128)S(1)} %bitcast.19), channel_id=1, source_target_pairs={{0,32},{32,64},{64,96},{96,128},{128,160},{160,192},{192,224},{1,3... | collective-permute-start | bytes 393224 | tf_op jit(solution)/shard_map/ppermute | solution.py:259
  55.1 39.7 %collective-permute-start.1 = (f32[32,8,128]{2,1,0:T(8,128)S(1)}, f32[32,8,128]{2,1,0:T(8,128)S(1)}, u32[]{:S(2)}, u32[]{:S(2)}) collective-permute-start(f32[32,8,128]{2,1,0:T(8,128)S(1)} %bitcast.18), channel_id=1, source_target_pairs={{32,0},{64,32},{96,64},{128,96},{160,128},{192,160},{224,192},{33,... | collective-permute-start | bytes 393224 | tf_op jit(solution)/shard_map/ppermute | solution.py:260
  94.8 0.7 copy-start.5
  95.5 21.4 %copy-start.1 = (f32[8,16384]{1,0:T(8,128)S(1)}, f32[8,16384]{1,0:T(8,128)}, u32[]{:S(2)}) copy-start(f32[8,16384]{1,0:T(8,128)} %attr_ref.3) | copy-start | bytes 1572868
  105.0 11.9 %copy-start.3 = (s32[16384]{0:T(1024)S(1)}, s32[16384]{0:T(1024)}, u32[]{:S(2)}) copy-start(s32[16384]{0:T(1024)} %param.7) | copy-start | bytes 196612

commit v2 on v1

--- a/solution.py
+++ b/solution.py
@@ -20,7 +20,8 @@
 CHUNK = 1024
 GCHUNK = 1024
 KF = 48
-SAME_UNROLL = 8
+KADJ = 64
+GROUP = 16
 ADJ_UNROLL = 8
 QROWS = 32
 MIB = 2**20
@@ -83,71 +84,67 @@
     high = rounded(v)
     rest = v - high
     norm = -0.5 * jnp.sum(jnp.where(six, v * v, 0.0), axis=0, keepdims=True)
-    radius = v[7:8]
-    x = jnp.where(lo3, jnp.broadcast_to(norm, (8, BLOCK)), jnp.broadcast_to(radius * radius, (8, BLOCK)))
-    p0 = rounded(x)
-    p1 = rounded(x - p0)
-    p2 = x - p0 - p1
+    n0 = rounded(norm)
+    n1 = rounded(norm - n0)
+    n2 = norm - n0 - n1
     k = jnp.where(lo3, row, row - 3)
-    own = jnp.where(six, jnp.where(k == 0, p0, jnp.where(k == 1, p1, p2)), 0.0)
-    one = jnp.ones((8, BLOCK), F32)
-    zero = jnp.zeros((8, BLOCK), F32)
-    mid3 = (row >= 3) & six
-    left = jnp.concatenate([high, high, rest, rest, own, jnp.where(six, one, zero)], axis=0)
+    parts = jnp.where(k == 0, n0, jnp.where(k == 1, n1, n2))
+    one = jnp.where(six, 1.0, 0.0)
     h6 = jnp.where(six, high, 0.0)
     m6 = jnp.where(six, rest, 0.0)
-    h7 = jnp.where(row == 7, 2.0 * high, 0.0)
-    m7 = jnp.where(row == 7, 2.0 * rest, 0.0)
-    arg = [h6, m6, h6, m6, jnp.where(lo3, one, zero), jnp.where(lo3, own, 0.0)]
-    reach = [h7, m7, h7, m7, jnp.where(mid3, one, zero), jnp.where(mid3, own, 0.0)]
-    right = jnp.concatenate([jnp.concatenate(arg, axis=0), jnp.concatenate(reach, axis=0)], axis=1)
+    zero = jnp.zeros((8, BLOCK), F32)
+    left = [high, rest, high, rest, jnp.where(lo3, parts, one), zero]
+    right = [h6, m6, m6, h6, jnp.where(lo3, one, jnp.where(six, parts, 0.0)), zero]
     return left, right
 
 
-def partner_form(v, left, j, xt_ref, mb_ref):
-    turned = jnp.concatenate([left, v], axis=0).T
-    xt_ref[j] = turned[:, :KF].astype(BF)
-    mb_ref[j] = jnp.broadcast_to(turned[:, KF + 6 : KF + 7], (BLOCK, BLOCK))
-
-
-def same_kernel(o_ref, mult_ref, out_ref, xt_ref, r_ref, mb_ref):
-    zero_right = jnp.zeros((KF, 2 * BLOCK), BF)
-    r_ref[0] = zero_right
-    r_ref[1] = zero_right
-
-    def build(j, carry):
-        v = o_ref[j]
-        left, right = forms(v)
-        r_ref[j + 2] = right.astype(BF)
-        partner_form(v, left, j, xt_ref, mb_ref)
-        return carry
-
-    lax.fori_loop(0, NBLK, build, 0, unroll=4)
-    lane = lax.broadcasted_iota(jnp.int32, (QROWS, BLOCK), 1)
-    sub = lax.broadcasted_iota(jnp.int32, (QROWS, BLOCK), 0)
-
-    def main(j, carry):
+def stacked(rows):
+    return jnp.concatenate(rows, axis=0).astype(BF)
+
+
+def spread_form():
+    row = lax.broadcasted_iota(jnp.int32, (KF, 2 * BLOCK), 0)
+    lane = lax.broadcasted_iota(jnp.int32, (KF, 2 * BLOCK), 1)
+    want = jnp.where(lane < BLOCK, 6, 7)
+    return jnp.where((row == want) | (row == want + 8), 1.0, 0.0).astype(BF)
+
+
+def same_kernel(o_ref, mult_ref, out_ref, xt0, xt1, r0, r1):
+    spread = spread_form()
+    shape8 = (8, BLOCK)
+    diff = lax.broadcasted_iota(jnp.int32, shape8, 1) - lax.broadcasted_iota(jnp.int32, shape8, 0)
+
+    def build(j, x, xt_ref, r_ref):
+        left, right = forms(o_ref[j])
+        r_ref[x + 2] = stacked(right)
+        xt_ref[x] = stacked(left).T
+
+    def main(j, x, xt_ref, r_ref, carry):
         f1, f2 = carry
         j1 = jnp.maximum(j - 1, 0)
         j2 = jnp.maximum(j - 2, 0)
-        rhs = jnp.concatenate([r_ref[j + 2], r_ref[j + 1], r_ref[j]], axis=1)
-        mass1 = o_ref[j1][6:7] * mult_ref[1, j]
-        mass2 = o_ref[j2][6:7] * mult_ref[0, j]
-        acc = [jnp.zeros((8, BLOCK), F32) for _ in range(3)]
+        own = [o_ref[j], o_ref[j1], o_ref[j2]]
+        radius = [jnp.broadcast_to(o[7:8], shape8) for o in own]
+        mass1 = own[1][6:7] * mult_ref[1, j]
+        mass2 = own[2][6:7] * mult_ref[0, j]
+        rhs = jnp.concatenate([r_ref[x + 2], r_ref[x + 1], r_ref[x], spread], axis=1)
+        acc = [jnp.zeros(shape8, F32) for _ in range(3)]
         rev = []
-        for q in range(BLOCK // QROWS):
-            at = slice(q * QROWS, (q + 1) * QROWS)
-            d = jnp.dot(xt_ref[j, at, :], rhs, preferred_element_type=F32)
-            mb = mb_ref[j, at, :]
-            w = []
-            for a in range(3):
-                low = a * 2 * BLOCK
-                e = jnp.exp2(d[:, low : low + BLOCK]) * d[:, low + BLOCK : low + 2 * BLOCK]
-                if a == 0:
-                    e = jnp.where(lane == sub + q * QROWS, 0.0, e)
-                w.append(e)
-                acc[a] = acc[a] + jnp.sum((e * mb).reshape(QROWS // 8, 8, BLOCK), axis=0)
-            rev.append(w[1] * mass1 + w[2] * mass2)
+        for q in range(0, BLOCK, QROWS):
+            d = jnp.dot(xt_ref[x, q : q + QROWS, :], rhs, preferred_element_type=F32)
+            for s in range(0, QROWS, 8):
+                z = d[s : s + 8]
+                mass = z[:, 3 * BLOCK : 4 * BLOCK]
+                reach = z[:, 4 * BLOCK : 5 * BLOCK]
+                w = []
+                for a in range(3):
+                    t = reach + radius[a]
+                    e = jnp.exp2(z[:, a * BLOCK : (a + 1) * BLOCK]) * (t * t)
+                    if a == 0:
+                        e = jnp.where(diff == q + s, 0.0, e)
+                    w.append(e)
+                    acc[a] = acc[a] + e * mass
+                rev.append(w[1] * mass1 + w[2] * mass2)
         back = jnp.sum(jnp.concatenate(rev, axis=0).T.reshape(BLOCK // 8, 8, BLOCK), axis=0)
         f0 = acc[0] * mult_ref[2, j] + back
         f1 = f1 + acc[1] * mult_ref[3, j1]
@@ -155,60 +152,111 @@
         out_ref[pl.ds(j2, 1), :] = jnp.sum(f2, axis=0, keepdims=True)
         return f0, f1
 
-    zero = jnp.zeros((8, BLOCK), F32)
-    f0, f1 = lax.fori_loop(0, NBLK, main, (zero, zero), unroll=SAME_UNROLL)
+    r0[0] = jnp.zeros((KF, BLOCK), BF)
+    r0[1] = jnp.zeros((KF, BLOCK), BF)
+    for x in range(GROUP):
+        build(x, x, xt0, r0)
+
+    def groups(u, carry):
+        for half, (xa, ra, xb, rb) in enumerate(((xt0, r0, xt1, r1), (xt1, r1, xt0, r0))):
+            base = (2 * u + half) * GROUP
+            later = jnp.minimum(base + GROUP, NBLK - GROUP)
+            rb[0] = ra[GROUP]
+            rb[1] = ra[GROUP + 1]
+            for x in range(GROUP):
+                build(later + x, x, xb, rb)
+                carry = main(base + x, x, xa, ra, carry)
+        return carry
+
+    zero = jnp.zeros(shape8, F32)
+    f0, f1 = lax.fori_loop(0, NBLK // (2 * GROUP), groups, (zero, zero))
     out_ref[NBLK - 1 : NBLK, :] = jnp.sum(f0, axis=0, keepdims=True)
     out_ref[NBLK - 2 : NBLK - 1, :] = jnp.sum(f1, axis=0, keepdims=True)
 
 
-def adj_kernel(o_ref, up_ref, down_ref, gain_ref, pairs_ref, count_ref, out_ref, xt_ref, r_ref, mb_ref):
-    out_ref[...] = gain_ref[...]
-
+def two(x):
+    high = rounded(x)
+    return high, x - high
+
+
+def adj_left(v):
+    left, _ = forms(v)
+    row = lax.broadcasted_iota(jnp.int32, (8, BLOCK), 0)
+    mass = v[6:7]
+    radius = v[7:8]
+    x = jnp.where(row < 4, mass, jnp.where(row < 8, mass * radius, 0.0))
+    h, m = two(x)
+    first = jnp.where(row % 4 < 2, h, m)
+    h, m = two(jnp.where(row < 4, mass * radius * radius, 0.0))
+    second = jnp.where(row % 4 < 2, h, m)
+    zero = jnp.zeros((8, BLOCK), F32)
+    return stacked(left[:5] + [first, second, zero])
+
+
+def adj_right(v):
+    _, right = forms(v)
+    row = lax.broadcasted_iota(jnp.int32, (8, BLOCK), 0)
+    radius = v[7:8]
+    h, m = two(jnp.where(row < 4, radius * radius, 2.0 * radius))
+    first = jnp.where(row % 2 == 0, h, m)
+    second = jnp.where((row < 4) & (row % 2 == 0), 1.0, 0.0)
+    zero = jnp.zeros((8, BLOCK), F32)
+    arg = right[:5] + [zero, zero, zero]
+    reach = [zero] * 5 + [first, second, zero]
+    return jnp.concatenate([stacked(arg), stacked(reach)], axis=1)
+
+
+def adj_kernel(o_ref, up_ref, down_ref, gain_ref, pairs_ref, list_ref, count_ref, out_ref, xt_ref, r_ref, found_ref):
     def build(j, carry):
         for half, ref in ((0, up_ref), (1, down_ref)):
-            v = ref[j]
-            left, _ = forms(v)
-            partner_form(v, left, j + half * EDGE, xt_ref, mb_ref)
-            _, right = forms(o_ref[j + half * (NBLK - EDGE)])
-            r_ref[j + half * EDGE] = right.astype(BF)
-        return carry
-
-    lax.fori_loop(0, EDGE, build, 0, unroll=2)
+            xt_ref[j + half * EDGE] = adj_left(ref[j]).T
+            r_ref[j + half * EDGE] = adj_right(o_ref[j + half * (NBLK - EDGE)])
+        return carry
+
+    lax.fori_loop(0, EDGE, build, 0, unroll=8)
     count = count_ref[0, 0]
+    found_ref[...] = jnp.zeros_like(found_ref)
 
     def main(u, carry):
-        found = []
         for x in range(ADJ_UNROLL):
             t = u * ADJ_UNROLL + x
-            i = jnp.clip(pairs_ref[0, t], 0, NBLK - 1)
+            i = pairs_ref[0, t]
             j = jnp.clip(pairs_ref[1, t], 0, 2 * EDGE - 1)
             k = jnp.clip(jnp.where(i < EDGE, i, i - (NBLK - 2 * EDGE)), 0, 2 * EDGE - 1)
             d = jnp.dot(xt_ref[j], r_ref[k], preferred_element_type=F32)
-            e = jnp.exp2(d[:, :BLOCK]) * d[:, BLOCK:] * mb_ref[j]
-            found.append((i, jnp.where(t < count, jnp.sum(e, axis=0, keepdims=True), 0.0)))
-        for i, e in found:
-            out_ref[pl.ds(i, 1), :] += e
+            e = jnp.exp2(d[:, :BLOCK]) * d[:, BLOCK:]
+            found_ref[pl.ds(t, 1), :] = jnp.sum(e, axis=0, keepdims=True)
         return carry
 
     lax.fori_loop(0, (count + ADJ_UNROLL - 1) // ADJ_UNROLL, main, 0)
+    live = lax.broadcasted_iota(jnp.int32, (1, PADJ), 1) < count
+    owner = onehot_rows(NBLK, jnp.where(live, list_ref[0:1, :], -1)).astype(BF)
+    h, m = two(found_ref[...])
+    h2, m2 = two(m)
+    total = gain_ref[...]
+    for part in (m2, h2, h):
+        total = total + jnp.dot(owner, part.astype(BF), preferred_element_type=F32)
+    out_ref[...] = total
 
 
 def gather_kernel(gain_ref, slot_ref, attr_ref, out_ref):
     turned = gain_ref[...].T
-    high = rounded(turned)
-    table = jnp.concatenate([high, turned - high], axis=1).astype(BF)
+    high, rest = two(turned)
+    table = jnp.concatenate([high, rest], axis=1).astype(BF)
+    number = lax.broadcasted_iota(jnp.int32, (NBLK, GCHUNK), 0).astype(F32).astype(BF)
 
     def step(s, carry):
         low = pl.multiple_of(s * GCHUNK, GCHUNK)
         slot = slot_ref[:, pl.ds(low, GCHUNK)]
-        block = onehot_rows(NBLK, slot >> 7).astype(BF)
+        block = number == (slot >> 7).astype(F32).astype(BF)
+        block = jnp.where(block, jnp.ones((), BF), jnp.zeros((), BF))
         z = jnp.dot(table, jnp.concatenate([block, block], axis=0), preferred_element_type=F32)
         lane = lax.broadcasted_iota(jnp.int32, (BLOCK, GCHUNK), 0) == (slot & 127)
         gain = jnp.sum(jnp.where(lane, z, 0.0), axis=0, keepdims=True)
         out_ref[:, pl.ds(low, GCHUNK)] = attr_ref[6:7, pl.ds(low, GCHUNK)] + RATE * gain
         return carry
 
-    lax.fori_loop(0, FLOC_DEV // GCHUNK, step, 0)
+    lax.fori_loop(0, FLOC_DEV // GCHUNK, step, 0, unroll=2)
 
 
 VMEM = pl.BlockSpec(memory_space=pltpu.VMEM)
@@ -264,9 +312,10 @@
         shape(NBLK, BLOCK),
         [VMEM, SMEM],
         [
-            pltpu.VMEM((NBLK, BLOCK, KF), BF),
-            pltpu.VMEM((NBLK + 2, KF, 2 * BLOCK), BF),
-            pltpu.VMEM((NBLK, BLOCK, BLOCK), F32),
+            pltpu.VMEM((GROUP, BLOCK, KF), BF),
+            pltpu.VMEM((GROUP, BLOCK, KF), BF),
+            pltpu.VMEM((GROUP + 2, KF, BLOCK), BF),
+            pltpu.VMEM((GROUP + 2, KF, BLOCK), BF),
         ],
         40_000_000_000,
         owned,
@@ -276,17 +325,18 @@
         adj_kernel,
         "adjacent_pairs",
         shape(NBLK, BLOCK),
-        [VMEM, VMEM, VMEM, VMEM, SMEM, SMEM],
+        [VMEM, VMEM, VMEM, VMEM, SMEM, VMEM, SMEM],
         [
-            pltpu.VMEM((2 * EDGE, BLOCK, KF), BF),
-            pltpu.VMEM((2 * EDGE, KF, 2 * BLOCK), BF),
-            pltpu.VMEM((2 * EDGE, BLOCK, BLOCK), F32),
+            pltpu.VMEM((2 * EDGE, BLOCK, KADJ), BF),
+            pltpu.VMEM((2 * EDGE, KADJ, 2 * BLOCK), BF),
+            pltpu.VMEM((PADJ, BLOCK), F32),
         ],
         10_000_000_000,
         owned,
         up,
         down,
         gain,
+        adj_pairs.reshape(2, PADJ),
         adj_pairs.reshape(2, PADJ),
         neighbour_pair_count,
     )

time: 125 us -> 99.8 us (0.80)
  Pallas kernels: 77 us -> 52.6 us
    pallas_call x4, Pallas kernels: 77 us -> 52.6 us  [call(): pl.pallas_call(kernel, out_shape=out, in_specs=ins, out_specs=jax.tree.ma...]
  transfers between devices with their start and end apart: 3 -> 3, of which waited for: 1 -> 1; matrix products, arithmetic and copies ran while one was open for 0% -> 0% of each run, Pallas kernels for 30% -> 19%
where the time goes in v2:
time: 99.8 us; the launch traced here: 98.8 us
  Pallas kernels  52.6 us (53%)
  waiting for transfers between devices  16.3 us (16%)
  starting transfers between devices  14.4 us (14%)
  blocking collectives  10.9 us (11%)
  local copies, waits for them, and re-layouts  3.25 us (3%)
  between operations  1.39 us (1%)
    pallas_call x4, Pallas kernels, call(): pl.pallas_call(kernel, out_shape=out, in_specs=ins, out_specs=jax.tree.ma...  52.6 us
    all_to_all x1, waiting for transfers between devices, body(): lax.all_to_all(send, 'tile', split_axis=0, concat_axis=0, tiled=True)  16.3 us
    all_to_all x1, blocking collectives, body(): lax.all_to_all(gain, 'tile', split_axis=0, concat_axis=0, tiled=True)  10.9 us
    all_to_all x1, starting transfers between devices, body(): lax.all_to_all(send, 'tile', split_axis=0, concat_axis=0, tiled=True)  7.71 us
    ppermute x1, starting transfers between devices, body(): lax.ppermute(owned[NBLK - EDGE:], 'seg', [(i, i + 1) for i in range(segs...  4.75 us
    unnamed x12, local copies, waits for them, and re-layouts  3.24 us
  transfers between devices with their start and end apart: 3, of which 1 were waited for; matrix products, arithmetic and copies ran while one was open for 0% of the time, Pallas kernels for 19%

profile of v2, /device:TPU:97, one launch (start us, length us, event | category | flops | bytes accessed | tf_op | source)
XLA Modules:
  0.0 98.8 jit_solution(1424253847709594400)
XLA Ops:
  0.7 0.0 copy-start
  0.7 1.0 %copy-done = f32[8,16384]{1,0:T(8,128)S(1)} copy-done((f32[8,16384]{1,0:T(8,128)S(1)}, f32[8,16384]{1,0:T(8,128)}, u32[]{:S(2)}) %copy-start) | copy-done | bytes 524312
  1.7 0.0 copy-start.2
  1.7 0.8 copy-done.2
  2.5 0.0 copy-start.4
  2.5 0.7 copy-done.4
  3.2 22.5 %scatter.1 = (f32[256,8,128]{2,1,0:T(8,128)}, f32[8,256]{1,0:T(8,128)S(1)}) custom-call(f32[8,16384]{1,0:T(8,128)S(1)} %copy-done, s32[1,16384]{1,0:T(1,128)S(1)} %bitcast.14, s32[2,1024]{1,0:T(2,128)S(1)} %bitcast.16, s32[1,1]{1,0:T(1,128)S(6)} %copy.7.count_ref), custom_call_target="tpu_custom_call" | custom-call | flops 17179869184 | bytes 2097152 | tf_op jit(solution)/shard_map/scatter/pallas_call | solution.py:267
  25.7 7.7 %all-to-all-start = ((f32[32,8,8,128]{3,2,1,0:T(8,128)}), f32[32,8,8,128]{3,2,1,0:T(8,128)S(1)}, u32[]{:S(2)}, u32[]{:S(2)}) async-start(f32[32,8,8,128]{3,2,1,0:T(8,128)} %bitcast.2), calls=%async_computation | async-start | bytes 2097152 | tf_op jit(solution)/shard_map/all_to_all | solution.py:305
  34.1 16.3 %all-to-all-done = f32[32,8,8,128]{3,2,1,0:T(8,128)S(1)} async-done(((f32[32,8,8,128]{3,2,1,0:T(8,128)}), f32[32,8,8,128]{3,2,1,0:T(8,128)S(1)}, u32[]{:S(2)}, u32[]{:S(2)}) %all-to-all-start) | async-done | bytes 1048608 | tf_op jit(solution)/shard_map/all_to_all | solution.py:305
  50.4 4.8 %collective-permute-start = (f32[32,8,128]{2,1,0:T(8,128)S(1)}, f32[32,8,128]{2,1,0:T(8,128)S(1)}, u32[]{:S(2)}, u32[]{:S(2)}) collective-permute-start(f32[32,8,128]{2,1,0:T(8,128)S(1)} %bitcast.20), channel_id=1, source_target_pairs={{0,32},{32,64},{64,96},{96,128},{128,160},{160,192},{192,224},{1,3... | collective-permute-start | bytes 393224 | tf_op jit(solution)/shard_map/ppermute | solution.py:307
  55.1 1.9 %collective-permute-start.1 = (f32[32,8,128]{2,1,0:T(8,128)S(1)}, f32[32,8,128]{2,1,0:T(8,128)S(1)}, u32[]{:S(2)}, u32[]{:S(2)}) collective-permute-start(f32[32,8,128]{2,1,0:T(8,128)S(1)} %bitcast.19), channel_id=1, source_target_pairs={{32,0},{64,32},{96,64},{128,96},{160,128},{192,160},{224,192},{33,... | collective-permute-start | bytes 393224 | tf_op jit(solution)/shard_map/ppermute | solution.py:308
  57.1 18.7 %same_pairs.1.gain_ref = f32[256,128]{1,0:T(8,128)S(1)} custom-call(f32[256,8,128]{2,1,0:T(8,128)S(1)} %bitcast.10, f32[8,256]{1,0:T(8,128)S(1)} %get-tuple-element.8.mult_ref), custom_call_target="tpu_custom_call" | custom-call | flops 40000000000 | bytes 2097152 | tf_op jit(solution)/shard_map/same_pairs/pallas_call | solution.py:267
  75.8 0.0 copy-start.5
  75.8 0.0 collective-permute-done.up_ref
  75.8 0.0 collective-permute-done.1.down_ref
  75.8 0.6 copy-done.5
  76.5 0.0 copy-start.1
  76.5 6.7 %adjacent_pairs.1 = f32[256,128]{1,0:T(8,128)S(1)} custom-call(f32[256,8,128]{2,1,0:T(8,128)S(1)} %bitcast.11, f32[32,8,128]{2,1,0:T(8,128)S(1)} %collective-permute-done.up_ref, f32[32,8,128]{2,1,0:T(8,128)S(1)} %collective-permute-done.1.down_ref, f32[256,128]{1,0:T(8,128)S(1)} %same_pairs.1.gain_ref, s32[2,128]{1,0:T(2,128)S(1)} %bitcast.17, ...), custom_call_target="tpu_custom_call" | custom-call | flops 10000000000 | bytes 2097152 | tf_op jit(solution)/shard_map/adjacent_pairs/pallas_call | solution.py:267
  83.2 0.0 copy-start.3
  83.3 10.9 %all_to_all.10 = f32[32,8,128]{2,1,0:T(8,128)S(1)} all-to-all(f32[32,8,128]{2,1,0:T(8,128)S(1)} %bitcast.12), channel_id=1, replica_groups=mesh['seg'=8,'tile'=32] {'tile'}, dimensions={0} | all-to-all | bytes 262144 | tf_op jit(solution)/shard_map/all_to_all | solution.py:344
  94.2 0.0 copy-done.1
  94.2 0.0 copy-done.3
  94.2 4.6 %final_gather.1 = f32[1,16384]{1,0:T(1,128)} custom-call(f32[256,128]{1,0:T(8,128)S(1)} %bitcast.13, s32[1,16384]{1,0:T(1,128)S(1)} %bitcast.15, f32[8,16384]{1,0:T(8,128)S(1)} %copy-done.1), custom_call_target="tpu_custom_call" | custom-call | flops 10000000000 | bytes 2097152 | tf_op jit(solution)/shard_map/final_gather/pallas_call | solution.py:267
  (1 shorter events, 0.0 us)
Async XLA Ops:
  0.7 1.0 %copy-start = (f32[8,16384]{1,0:T(8,128)S(1)}, f32[8,16384]{1,0:T(8,128)}, u32[]{:S(2)}) copy-start(f32[8,16384]{1,0:T(8,128)} %attr_ref.3) | copy-start | bytes 1572868
  1.7 0.8 copy-start.2
  2.5 0.7 copy-start.4
  25.7 24.6 %all-to-all-start = ((f32[32,8,8,128]{3,2,1,0:T(8,128)}), f32[32,8,8,128]{3,2,1,0:T(8,128)S(1)}, u32[]{:S(2)}, u32[]{:S(2)}) async-start(f32[32,8,8,128]{3,2,1,0:T(8,128)} %bitcast.2), calls=%async_computation | async-start | bytes 2097152 | tf_op jit(solution)/shard_map/all_to_all | solution.py:305
  50.4 25.4 %collective-permute-start = (f32[32,8,128]{2,1,0:T(8,128)S(1)}, f32[32,8,128]{2,1,0:T(8,128)S(1)}, u32[]{:S(2)}, u32[]{:S(2)}) collective-permute-start(f32[32,8,128]{2,1,0:T(8,128)S(1)} %bitcast.20), channel_id=1, source_target_pairs={{0,32},{32,64},{64,96},{96,128},{128,160},{160,192},{192,224},{1,3... | collective-permute-start | bytes 393224 | tf_op jit(solution)/shard_map/ppermute | solution.py:307
  55.1 20.7 %collective-permute-start.1 = (f32[32,8,128]{2,1,0:T(8,128)S(1)}, f32[32,8,128]{2,1,0:T(8,128)S(1)}, u32[]{:S(2)}, u32[]{:S(2)}) collective-permute-start(f32[32,8,128]{2,1,0:T(8,128)S(1)} %bitcast.19), channel_id=1, source_target_pairs={{32,0},{64,32},{96,64},{128,96},{160,128},{192,160},{224,192},{33,... | collective-permute-start | bytes 393224 | tf_op jit(solution)/shard_map/ppermute | solution.py:308
  75.8 0.7 copy-start.5
  76.5 17.7 %copy-start.1 = (f32[8,16384]{1,0:T(8,128)S(1)}, f32[8,16384]{1,0:T(8,128)}, u32[]{:S(2)}) copy-start(f32[8,16384]{1,0:T(8,128)} %attr_ref.3) | copy-start | bytes 1572868
  83.2 10.9 %copy-start.3 = (s32[16384]{0:T(1024)S(1)}, s32[16384]{0:T(1024)}, u32[]{:S(2)}) copy-start(s32[16384]{0:T(1024)} %param.7) | copy-start | bytes 196612

commit v3 on v2

--- a/solution.py
+++ b/solution.py
@@ -22,7 +22,7 @@
 KF = 48
 KADJ = 64
 GROUP = 16
-ADJ_UNROLL = 8
+ADJ_UNROLL = 32
 QROWS = 32
 MIB = 2**20
 BF = jnp.bfloat16
@@ -38,7 +38,20 @@
     return jnp.where(lax.broadcasted_iota(jnp.int32, shape, 0) == index, 1.0, 0.0)
 
 
-def scatter_kernel(attr_ref, slot_ref, pairs_ref, count_ref, out_ref, mult_ref, y_ref, b_ref, acc_ref):
+def fetch(sources, targets, sems):
+    copies = [
+        pltpu.make_async_copy(source, target, sems.at[n])
+        for n, (source, target) in enumerate(zip(sources, targets))
+    ]
+    for copy in copies:
+        copy.start()
+    return copies
+
+
+def scatter_kernel(attr_hbm, slot_hbm, pairs_hbm, count_ref, out_ref, mult_ref, attr_ref, slot_ref, pairs_ref, sems, y_ref, b_ref, acc_ref):
+    copies = fetch((attr_hbm, slot_hbm, pairs_hbm), (attr_ref, slot_ref, pairs_ref), sems)
+    acc_ref[...] = jnp.zeros_like(acc_ref)
+    copies[2].wait()
     first = pairs_ref[0:1, :]
     offset = pairs_ref[1:2, :] - first + 2
     live = lax.broadcasted_iota(jnp.int32, (1, PSAME), 1) < count_ref[0, 0]
@@ -71,7 +84,8 @@
         )
         return carry
 
-    acc_ref[...] = jnp.zeros_like(acc_ref)
+    copies[0].wait()
+    copies[1].wait()
     lax.fori_loop(0, FLOC_DEV // CHUNK, step, 0)
     for a in range(ATTR):
         out_ref[:, a, :] = acc_ref[a * BLOCK : (a + 1) * BLOCK, :].T
@@ -261,6 +275,7 @@
 
 VMEM = pl.BlockSpec(memory_space=pltpu.VMEM)
 SMEM = pl.BlockSpec(memory_space=pltpu.SMEM)
+HBM = pl.BlockSpec(memory_space=pltpu.HBM)
 
 
 def call(kernel, name, out, ins, scratch, cost, *args):
@@ -270,7 +285,7 @@
         in_specs=ins,
         out_specs=jax.tree.map(lambda _: VMEM, out),
         scratch_shapes=scratch,
-        compiler_params=pltpu.CompilerParams(vmem_limit_bytes=52 * MIB),
+        compiler_params=pltpu.CompilerParams(vmem_limit_bytes=(60 if name == "scatter" else 52) * MIB),
         cost_estimate=pl.CostEstimate(flops=cost, bytes_accessed=2 * MIB, transcendentals=0),
         name=name,
     )(*args)
@@ -289,8 +304,12 @@
         scatter_kernel,
         "scatter",
         (shape(NBLK, ATTR, BLOCK), shape(8, NBLK)),
-        [VMEM, VMEM, VMEM, SMEM],
+        [HBM, HBM, HBM, SMEM],
         [
+            pltpu.VMEM((ATTR, FLOC_DEV), F32),
+            pltpu.VMEM((1, FLOC_DEV), jnp.int32),
+            pltpu.VMEM((2, PSAME), jnp.int32),
+            pltpu.SemaphoreType.DMA((3,)),
             pltpu.VMEM((ATTR * BLOCK, 2 * CHUNK), BF),
             pltpu.VMEM((NBLK, 2 * CHUNK), BF),
             pltpu.VMEM((ATTR * BLOCK, NBLK), F32),

time: 99.8 us -> 96.6 us (0.968)
  local copies, waits for them, and re-layouts: 3.25 us -> 0.69 us
  Pallas kernels: 52.6 us -> 51.5 us
    unnamed x12 -> x8, local copies, waits for them, and re-layouts: 3.24 us -> 0.67 us
    pallas_call x4, Pallas kernels: 52.6 us -> 51.5 us  [call(): pl.pallas_call(kernel, out_shape=out, in_specs=ins, out_specs=jax.tree.ma...]
where the time goes in v3:
time: 96.6 us; the launch traced here: 95.9 us
  Pallas kernels  51.5 us (53%)
  waiting for transfers between devices  16.3 us (17%)
  starting transfers between devices  14.5 us (15%)
  blocking collectives  11.6 us (12%)
  between operations  1.4 us (1%)
    pallas_call x4, Pallas kernels, call(): pl.pallas_call(kernel, out_shape=out, in_specs=ins, out_specs=jax.tree.ma...  51.5 us
    all_to_all x1, waiting for transfers between devices, body(): lax.all_to_all(send, 'tile', split_axis=0, concat_axis=0, tiled=True)  16.3 us
    all_to_all x1, blocking collectives, body(): lax.all_to_all(gain, 'tile', split_axis=0, concat_axis=0, tiled=True)  11.6 us
    all_to_all x1, starting transfers between devices, body(): lax.all_to_all(send, 'tile', split_axis=0, concat_axis=0, tiled=True)  7.83 us
    ppermute x1, starting transfers between devices, body(): lax.ppermute(owned[NBLK - EDGE:], 'seg', [(i, i + 1) for i in range(segs...  4.71 us
  transfers between devices with their start and end apart: 3, of which 1 were waited for; matrix products, arithmetic and copies ran while one was open for 0% of the time, Pallas kernels for 19%

profile of v3, /device:TPU:97, one launch (start us, length us, event | category | flops | bytes accessed | tf_op | source)
XLA Modules:
  0.0 95.9 jit_solution(8255225278491184416)
XLA Ops:
  0.7 23.4 %scatter.1 = (f32[256,8,128]{2,1,0:T(8,128)}, f32[8,256]{1,0:T(8,128)}) custom-call(f32[8,16384]{1,0:T(8,128)} %attr_ref.1, s32[1,16384]{1,0:T(1,128)} %bitcast.14, s32[2,1024]{1,0:T(2,128)} %bitcast.21, s32[1,1]{1,0:T(1,128)S(6)} %copy.7.count_ref), custom_call_target="tpu_custom_call" | custom-call | flops 17179869184 | bytes 2097152 | tf_op jit(solution)/shard_map/scatter/pallas_call | solution.py:282
  24.0 7.8 %all-to-all-start = ((f32[32,8,8,128]{3,2,1,0:T(8,128)}), f32[32,8,8,128]{3,2,1,0:T(8,128)S(1)}, u32[]{:S(2)}, u32[]{:S(2)}) async-start(f32[32,8,8,128]{3,2,1,0:T(8,128)} %bitcast.18), calls=%async_computation | async-start | bytes 2097152 | tf_op jit(solution)/shard_map/all_to_all | solution.py:324
  32.5 16.3 %all-to-all-done = f32[32,8,8,128]{3,2,1,0:T(8,128)S(1)} async-done(((f32[32,8,8,128]{3,2,1,0:T(8,128)}), f32[32,8,8,128]{3,2,1,0:T(8,128)S(1)}, u32[]{:S(2)}, u32[]{:S(2)}) %all-to-all-start) | async-done | bytes 1048608 | tf_op jit(solution)/shard_map/all_to_all | solution.py:324
  48.8 0.0 copy-start.3
  48.8 4.7 %collective-permute-start = (f32[32,8,128]{2,1,0:T(8,128)S(1)}, f32[32,8,128]{2,1,0:T(8,128)S(1)}, u32[]{:S(2)}, u32[]{:S(2)}) collective-permute-start(f32[32,8,128]{2,1,0:T(8,128)S(1)} %bitcast.20), channel_id=1, source_target_pairs={{0,32},{32,64},{64,96},{96,128},{128,160},{160,192},{192,224},{1,3... | collective-permute-start | bytes 393224 | tf_op jit(solution)/shard_map/ppermute | solution.py:326
  53.5 1.9 %collective-permute-start.1 = (f32[32,8,128]{2,1,0:T(8,128)S(1)}, f32[32,8,128]{2,1,0:T(8,128)S(1)}, u32[]{:S(2)}, u32[]{:S(2)}) collective-permute-start(f32[32,8,128]{2,1,0:T(8,128)S(1)} %bitcast.19), channel_id=1, source_target_pairs={{32,0},{64,32},{96,64},{128,96},{160,128},{192,160},{224,192},{33,... | collective-permute-start | bytes 393224 | tf_op jit(solution)/shard_map/ppermute | solution.py:327
  55.5 0.0 copy-done.3
  55.5 18.7 %same_pairs.1.gain_ref = f32[256,128]{1,0:T(8,128)S(1)} custom-call(f32[256,8,128]{2,1,0:T(8,128)S(1)} %bitcast.10, f32[8,256]{1,0:T(8,128)S(1)} %copy-done.3), custom_call_target="tpu_custom_call" | custom-call | flops 40000000000 | bytes 2097152 | tf_op jit(solution)/shard_map/same_pairs/pallas_call | solution.py:282
  74.2 0.0 copy-start.2
  74.2 0.0 collective-permute-done.up_ref
  74.2 0.0 collective-permute-done.1.down_ref
  74.2 0.6 copy-done.2
  74.9 0.0 copy-start
  74.9 4.8 %adjacent_pairs.1 = f32[256,128]{1,0:T(8,128)S(1)} custom-call(f32[256,8,128]{2,1,0:T(8,128)S(1)} %bitcast.11, f32[32,8,128]{2,1,0:T(8,128)S(1)} %collective-permute-done.up_ref, f32[32,8,128]{2,1,0:T(8,128)S(1)} %collective-permute-done.1.down_ref, f32[256,128]{1,0:T(8,128)S(1)} %same_pairs.1.gain_ref, s32[2,128]{1,0:T(2,128)S(1)} %bitcast.16, ...), custom_call_target="tpu_custom_call" | custom-call | flops 10000000000 | bytes 2097152 | tf_op jit(solution)/shard_map/adjacent_pairs/pallas_call | solution.py:282
  79.7 0.0 copy-start.1
  79.7 11.6 %all_to_all.10 = f32[32,8,128]{2,1,0:T(8,128)S(1)} all-to-all(f32[32,8,128]{2,1,0:T(8,128)S(1)} %bitcast.12), channel_id=1, replica_groups=mesh['seg'=8,'tile'=32] {'tile'}, dimensions={0} | all-to-all | bytes 262144 | tf_op jit(solution)/shard_map/all_to_all | solution.py:363
  91.2 0.0 copy-done
  91.2 0.0 copy-done.1
  91.3 4.6 %final_gather.1 = f32[1,16384]{1,0:T(1,128)} custom-call(f32[256,128]{1,0:T(8,128)S(1)} %bitcast.13, s32[1,16384]{1,0:T(1,128)S(1)} %bitcast.15, f32[8,16384]{1,0:T(8,128)S(1)} %copy-done), custom_call_target="tpu_custom_call" | custom-call | flops 10000000000 | bytes 2097152 | tf_op jit(solution)/shard_map/final_gather/pallas_call | solution.py:282
  (1 shorter events, 0.0 us)
Async XLA Ops:
  24.0 24.7 %all-to-all-start = ((f32[32,8,8,128]{3,2,1,0:T(8,128)}), f32[32,8,8,128]{3,2,1,0:T(8,128)S(1)}, u32[]{:S(2)}, u32[]{:S(2)}) async-start(f32[32,8,8,128]{3,2,1,0:T(8,128)} %bitcast.18), calls=%async_computation | async-start | bytes 2097152 | tf_op jit(solution)/shard_map/all_to_all | solution.py:324
  48.8 6.7 %copy-start.3 = (f32[8,256]{1,0:T(8,128)S(1)}, f32[8,256]{1,0:T(8,128)}, u32[]{:S(2)}) copy-start(f32[8,256]{1,0:T(8,128)} %get-tuple-element.8.mult_ref) | copy-start | bytes 24580
  48.8 25.4 %collective-permute-start = (f32[32,8,128]{2,1,0:T(8,128)S(1)}, f32[32,8,128]{2,1,0:T(8,128)S(1)}, u32[]{:S(2)}, u32[]{:S(2)}) collective-permute-start(f32[32,8,128]{2,1,0:T(8,128)S(1)} %bitcast.20), channel_id=1, source_target_pairs={{0,32},{32,64},{64,96},{96,128},{128,160},{160,192},{192,224},{1,3... | collective-permute-start | bytes 393224 | tf_op jit(solution)/shard_map/ppermute | solution.py:326
  53.5 20.7 %collective-permute-start.1 = (f32[32,8,128]{2,1,0:T(8,128)S(1)}, f32[32,8,128]{2,1,0:T(8,128)S(1)}, u32[]{:S(2)}, u32[]{:S(2)}) collective-permute-start(f32[32,8,128]{2,1,0:T(8,128)S(1)} %bitcast.19), channel_id=1, source_target_pairs={{32,0},{64,32},{96,64},{128,96},{160,128},{192,160},{224,192},{33,... | collective-permute-start | bytes 393224 | tf_op jit(solution)/shard_map/ppermute | solution.py:327
  74.2 0.7 copy-start.2
  74.9 16.4 %copy-start = (f32[8,16384]{1,0:T(8,128)S(1)}, f32[8,16384]{1,0:T(8,128)}, u32[]{:S(2)}) copy-start(f32[8,16384]{1,0:T(8,128)} %attr_ref.1) | copy-start | bytes 1572868
  79.7 11.6 %copy-start.1 = (s32[16384]{0:T(1024)S(1)}, s32[16384]{0:T(1024)}, u32[]{:S(2)}) copy-start(s32[16384]{0:T(1024)} %param.7) | copy-start | bytes 196612

commit v4 on v3

--- a/solution.py
+++ b/solution.py
@@ -17,7 +17,7 @@
 PSAME = 1024
 PADJ = 128
 SCALE = float(np.sqrt(np.log2(np.e)))
-CHUNK = 1024
+CHUNK = 2048
 GCHUNK = 1024
 KF = 48
 KADJ = 64
@@ -48,8 +48,13 @@
     return copies
 
 
-def scatter_kernel(attr_hbm, slot_hbm, pairs_hbm, count_ref, out_ref, mult_ref, attr_ref, slot_ref, pairs_ref, sems, y_ref, b_ref, acc_ref):
-    copies = fetch((attr_hbm, slot_hbm, pairs_hbm), (attr_ref, slot_ref, pairs_ref), sems)
+def scatter_kernel(
+    attr_hbm, slot_hbm, pairs_hbm, adj_hbm, count_ref, out_ref, mult_ref, adj_ref,
+    attr_ref, slot_ref, pairs_ref, sems, y0, y1, b0, b1, acc_ref,
+):
+    copies = fetch(
+        (attr_hbm, slot_hbm, pairs_hbm, adj_hbm), (attr_ref, slot_ref, pairs_ref, adj_ref), sems
+    )
     acc_ref[...] = jnp.zeros_like(acc_ref)
     copies[2].wait()
     first = pairs_ref[0:1, :]
@@ -62,31 +67,43 @@
         (((1,), (1,)), ((), ())),
         preferred_element_type=F32,
     )
+    number = lax.broadcasted_iota(jnp.int32, (NBLK, CHUNK), 0).astype(F32).astype(BF)
     row = lax.broadcasted_iota(jnp.int32, (ATTR, CHUNK), 0)
-
-    def step(s, carry):
+    zero = jnp.zeros((), BF)
+    chunks = FLOC_DEV // CHUNK
+
+    def spread(s, y_ref, b_ref):
         low = pl.multiple_of(s * CHUNK, CHUNK)
         slot = slot_ref[:, pl.ds(low, CHUNK)]
-        block = onehot_rows(NBLK, slot >> 7).astype(BF)
+        block = jnp.where(number == (slot >> 7).astype(F32).astype(BF), jnp.ones((), BF), zero)
         b_ref[:, :CHUNK] = block
         b_ref[:, CHUNK:] = block
-        lane = lax.broadcasted_iota(jnp.int32, (BLOCK, CHUNK), 0) == (slot & 127)
+        lane = number[:BLOCK] == (slot & 127).astype(F32).astype(BF)
         value = attr_ref[:, pl.ds(low, CHUNK)]
         value = jnp.where(row < 6, value * SCALE, value)
-        high = rounded(value)
-        rest = value - high
+        high = value.astype(BF)
+        rest = (value - high.astype(F32)).astype(BF)
         for a in range(ATTR):
             at = slice(a * BLOCK, (a + 1) * BLOCK)
-            y_ref[at, :CHUNK] = jnp.where(lane, high[a : a + 1], 0.0).astype(BF)
-            y_ref[at, CHUNK:] = jnp.where(lane, rest[a : a + 1], 0.0).astype(BF)
+            y_ref[at, :CHUNK] = jnp.where(lane, high[a : a + 1], zero)
+            y_ref[at, CHUNK:] = jnp.where(lane, rest[a : a + 1], zero)
+
+    def place(y_ref, b_ref):
         acc_ref[...] += lax.dot_general(
             y_ref[...], b_ref[...], (((1,), (1,)), ((), ())), preferred_element_type=F32
         )
+
+    def step(u, carry):
+        spread(2 * u + 1, y1, b1)
+        place(y0, b0)
+        spread(jnp.minimum(2 * u + 2, chunks - 1), y0, b0)
+        place(y1, b1)
         return carry
 
-    copies[0].wait()
-    copies[1].wait()
-    lax.fori_loop(0, FLOC_DEV // CHUNK, step, 0)
+    for n in (0, 1, 3):
+        copies[n].wait()
+    spread(0, y0, b0)
+    lax.fori_loop(0, chunks // 2, step, 0)
     for a in range(ATTR):
         out_ref[:, a, :] = acc_ref[a * BLOCK : (a + 1) * BLOCK, :].T
 
@@ -300,17 +317,19 @@
     cap_blocks = NBLK // tiles
     segs = lax.axis_size("seg")
     slot_row = floc_slot.reshape(1, FLOC_DEV)
-    send, mult = call(
+    send, mult, adj_list = call(
         scatter_kernel,
         "scatter",
-        (shape(NBLK, ATTR, BLOCK), shape(8, NBLK)),
-        [HBM, HBM, HBM, SMEM],
+        (shape(NBLK, ATTR, BLOCK), shape(8, NBLK), jax.ShapeDtypeStruct((2, PADJ), jnp.int32)),
+        [HBM, HBM, HBM, HBM, SMEM],
         [
             pltpu.VMEM((ATTR, FLOC_DEV), F32),
             pltpu.VMEM((1, FLOC_DEV), jnp.int32),
             pltpu.VMEM((2, PSAME), jnp.int32),
-            pltpu.SemaphoreType.DMA((3,)),
+            pltpu.SemaphoreType.DMA((4,)),
             pltpu.VMEM((ATTR * BLOCK, 2 * CHUNK), BF),
+            pltpu.VMEM((ATTR * BLOCK, 2 * CHUNK), BF),
+            pltpu.VMEM((NBLK, 2 * CHUNK), BF),
             pltpu.VMEM((NBLK, 2 * CHUNK), BF),
             pltpu.VMEM((ATTR * BLOCK, NBLK), F32),
         ],
@@ -318,6 +337,7 @@
         floc_attr,
         slot_row,
         same_pairs.reshape(2, PSAME),
+        adj_pairs.reshape(2, PADJ),
         same_count,
     )
     send = send.reshape(tiles, cap_blocks, ATTR, BLOCK)
@@ -355,8 +375,8 @@
         up,
         down,
         gain,
-        adj_pairs.reshape(2, PADJ),
-        adj_pairs.reshape(2, PADJ),
+        adj_list,
+        adj_list,
         neighbour_pair_count,
     )
     gain = gain.reshape(tiles, cap_blocks, BLOCK)

time: 96.6 us -> 95.3 us (0.987)
  Pallas kernels: 51.5 us -> 48.9 us
  blocking collectives: 11.6 us -> 13.3 us
    pallas_call x4, Pallas kernels: 51.5 us -> 48.9 us  [call(): pl.pallas_call(kernel, out_shape=out, in_specs=ins, out_specs=jax.tree.ma...]
    all_to_all x1, blocking collectives: 11.6 us -> 13.3 us  [body(): lax.all_to_all(gain, 'tile', split_axis=0, concat_axis=0, tiled=True)]
  transfers between devices with their start and end apart: 3 -> 3, of which waited for: 1 -> 1; matrix products, arithmetic and copies ran while one was open for 0% -> 0% of each run, Pallas kernels for 19% -> 20%
where the time goes in v4:
time: 95.3 us; the launch traced here: 94.9 us
  Pallas kernels  48.9 us (51%)
  waiting for transfers between devices  16.3 us (17%)
  starting transfers between devices  14.4 us (15%)
  blocking collectives  13.3 us (14%)
  between operations  1.4 us (1%)
    pallas_call x4, Pallas kernels, call(): pl.pallas_call(kernel, out_shape=out, in_specs=ins, out_specs=jax.tree.ma...  48.9 us
    all_to_all x1, waiting for transfers between devices, body(): lax.all_to_all(send, 'tile', split_axis=0, concat_axis=0, tiled=True)  16.3 us
    all_to_all x1, blocking collectives, body(): lax.all_to_all(gain, 'tile', split_axis=0, concat_axis=0, tiled=True)  13.3 us
    all_to_all x1, starting transfers between devices, body(): lax.all_to_all(send, 'tile', split_axis=0, concat_axis=0, tiled=True)  7.77 us
    ppermute x1, starting transfers between devices, body(): lax.ppermute(owned[NBLK - EDGE:], 'seg', [(i, i + 1) for i in range(segs...  4.76 us
    ppermute x1, starting transfers between devices, body(): lax.ppermute(owned[:EDGE], 'seg', [(i + 1, i) for i in range(segs - 1)])  1.92 us
  transfers between devices with their start and end apart: 3, of which 1 were waited for; matrix products, arithmetic and copies ran while one was open for 0% of the time, Pallas kernels for 20%

profile of v4, /device:TPU:97, one launch (start us, length us, event | category | flops | bytes accessed | tf_op | source)
XLA Modules:
  0.0 94.9 jit_solution(8559860841182968848)
XLA Ops:
  0.7 22.2 %scatter.1 = (f32[256,8,128]{2,1,0:T(8,128)}, f32[8,256]{1,0:T(8,128)}, s32[2,128]{1,0:T(2,128)}) custom-call(f32[8,16384]{1,0:T(8,128)} %attr_ref.1, s32[1,16384]{1,0:T(1,128)} %bitcast.14, s32[2,1024]{1,0:T(2,128)} %bitcast.19, s32[2,128]{1,0:T(2,128)} %bitcast.20, s32[1,1]{1,0:T(1,128)S(6)} %copy.7.count_ref), custom_call_target="tpu_custom_call" | custom-call | flops 17179869184 | bytes 2097152 | tf_op jit(solution)/shard_map/scatter/pallas_call | solution.py:299
  22.8 7.8 %all-to-all-start = ((f32[32,8,8,128]{3,2,1,0:T(8,128)}), f32[32,8,8,128]{3,2,1,0:T(8,128)S(1)}, u32[]{:S(2)}, u32[]{:S(2)}) async-start(f32[32,8,8,128]{3,2,1,0:T(8,128)} %bitcast.16), calls=%async_computation | async-start | bytes 2097152 | tf_op jit(solution)/shard_map/all_to_all | solution.py:344
  31.3 16.3 %all-to-all-done = f32[32,8,8,128]{3,2,1,0:T(8,128)S(1)} async-done(((f32[32,8,8,128]{3,2,1,0:T(8,128)}), f32[32,8,8,128]{3,2,1,0:T(8,128)S(1)}, u32[]{:S(2)}, u32[]{:S(2)}) %all-to-all-start) | async-done | bytes 1048608 | tf_op jit(solution)/shard_map/all_to_all | solution.py:344
  47.6 0.0 copy-start.2
  47.6 4.8 %collective-permute-start = (f32[32,8,128]{2,1,0:T(8,128)S(1)}, f32[32,8,128]{2,1,0:T(8,128)S(1)}, u32[]{:S(2)}, u32[]{:S(2)}) collective-permute-start(f32[32,8,128]{2,1,0:T(8,128)S(1)} %bitcast.18), channel_id=1, source_target_pairs={{0,32},{32,64},{64,96},{96,128},{128,160},{160,192},{192,224},{1,3... | collective-permute-start | bytes 393224 | tf_op jit(solution)/shard_map/ppermute | solution.py:346
  52.3 1.9 %collective-permute-start.1 = (f32[32,8,128]{2,1,0:T(8,128)S(1)}, f32[32,8,128]{2,1,0:T(8,128)S(1)}, u32[]{:S(2)}, u32[]{:S(2)}) collective-permute-start(f32[32,8,128]{2,1,0:T(8,128)S(1)} %bitcast.17), channel_id=1, source_target_pairs={{32,0},{64,32},{96,64},{128,96},{160,128},{192,160},{224,192},{33,... | collective-permute-start | bytes 393224 | tf_op jit(solution)/shard_map/ppermute | solution.py:347
  54.3 0.0 copy-done.2
  54.3 18.7 %same_pairs.1.gain_ref = f32[256,128]{1,0:T(8,128)S(1)} custom-call(f32[256,8,128]{2,1,0:T(8,128)S(1)} %bitcast.10, f32[8,256]{1,0:T(8,128)S(1)} %copy-done.2), custom_call_target="tpu_custom_call" | custom-call | flops 40000000000 | bytes 2097152 | tf_op jit(solution)/shard_map/same_pairs/pallas_call | solution.py:299
  72.9 0.0 copy-start.3
  73.0 0.0 collective-permute-done.up_ref
  73.0 0.0 collective-permute-done.1.down_ref
  73.0 0.6 copy-done.3
  73.6 0.0 copy-start
  73.6 3.4 %adjacent_pairs.1 = f32[256,128]{1,0:T(8,128)S(1)} custom-call(f32[256,8,128]{2,1,0:T(8,128)S(1)} %bitcast.11, f32[32,8,128]{2,1,0:T(8,128)S(1)} %collective-permute-done.up_ref, f32[32,8,128]{2,1,0:T(8,128)S(1)} %collective-permute-done.1.down_ref, f32[256,128]{1,0:T(8,128)S(1)} %same_pairs.1.gain_ref, s32[2,128]{1,0:T(2,128)S(1)} %copy-done.3, ...), custom_call_target="tpu_custom_call" | custom-call | flops 10000000000 | bytes 2097152 | tf_op jit(solution)/shard_map/adjacent_pairs/pallas_call | solution.py:299
  77.0 0.0 copy-start.1
  77.0 13.3 %all_to_all.10 = f32[32,8,128]{2,1,0:T(8,128)S(1)} all-to-all(f32[32,8,128]{2,1,0:T(8,128)S(1)} %bitcast.12), channel_id=1, replica_groups=mesh['seg'=8,'tile'=32] {'tile'}, dimensions={0} | all-to-all | bytes 262144 | tf_op jit(solution)/shard_map/all_to_all | solution.py:383
  90.3 0.0 copy-done
  90.3 0.0 copy-done.1
  90.3 4.6 %final_gather.1 = f32[1,16384]{1,0:T(1,128)} custom-call(f32[256,128]{1,0:T(8,128)S(1)} %bitcast.13, s32[1,16384]{1,0:T(1,128)S(1)} %bitcast.15, f32[8,16384]{1,0:T(8,128)S(1)} %copy-done), custom_call_target="tpu_custom_call" | custom-call | flops 10000000000 | bytes 2097152 | tf_op jit(solution)/shard_map/final_gather/pallas_call | solution.py:299
  (1 shorter events, 0.0 us)
Async XLA Ops:
  22.8 24.7 %all-to-all-start = ((f32[32,8,8,128]{3,2,1,0:T(8,128)}), f32[32,8,8,128]{3,2,1,0:T(8,128)S(1)}, u32[]{:S(2)}, u32[]{:S(2)}) async-start(f32[32,8,8,128]{3,2,1,0:T(8,128)} %bitcast.16), calls=%async_computation | async-start | bytes 2097152 | tf_op jit(solution)/shard_map/all_to_all | solution.py:344
  47.6 6.7 %copy-start.2 = (f32[8,256]{1,0:T(8,128)S(1)}, f32[8,256]{1,0:T(8,128)}, u32[]{:S(2)}) copy-start(f32[8,256]{1,0:T(8,128)} %get-tuple-element.9.mult_ref) | copy-start | bytes 24580
  47.6 25.4 %collective-permute-start = (f32[32,8,128]{2,1,0:T(8,128)S(1)}, f32[32,8,128]{2,1,0:T(8,128)S(1)}, u32[]{:S(2)}, u32[]{:S(2)}) collective-permute-start(f32[32,8,128]{2,1,0:T(8,128)S(1)} %bitcast.18), channel_id=1, source_target_pairs={{0,32},{32,64},{64,96},{96,128},{128,160},{160,192},{192,224},{1,3... | collective-permute-start | bytes 393224 | tf_op jit(solution)/shard_map/ppermute | solution.py:346
  52.3 20.6 %collective-permute-start.1 = (f32[32,8,128]{2,1,0:T(8,128)S(1)}, f32[32,8,128]{2,1,0:T(8,128)S(1)}, u32[]{:S(2)}, u32[]{:S(2)}) collective-permute-start(f32[32,8,128]{2,1,0:T(8,128)S(1)} %bitcast.17), channel_id=1, source_target_pairs={{32,0},{64,32},{96,64},{128,96},{160,128},{192,160},{224,192},{33,... | collective-permute-start | bytes 393224 | tf_op jit(solution)/shard_map/ppermute | solution.py:347
  72.9 0.6 copy-start.3
  73.6 16.7 %copy-start = (f32[8,16384]{1,0:T(8,128)S(1)}, f32[8,16384]{1,0:T(8,128)}, u32[]{:S(2)}) copy-start(f32[8,16384]{1,0:T(8,128)} %attr_ref.1) | copy-start | bytes 1572868
  77.0 13.3 %copy-start.1 = (s32[16384]{0:T(1024)S(1)}, s32[16384]{0:T(1024)}, u32[]{:S(2)}) copy-start(s32[16384]{0:T(1024)} %param.7) | copy-start | bytes 196612

commit v5 on v4

--- a/solution.py
+++ b/solution.py
@@ -22,7 +22,7 @@
 KF = 48
 KADJ = 64
 GROUP = 16
-ADJ_UNROLL = 32
+ADJ_UNROLL = 64
 QROWS = 32
 MIB = 2**20
 BF = jnp.bfloat16
@@ -140,7 +140,8 @@
     return jnp.where((row == want) | (row == want + 8), 1.0, 0.0).astype(BF)
 
 
-def same_kernel(o_ref, mult_ref, out_ref, xt0, xt1, r0, r1):
+def same_kernel(o_ref, mult_ref, list_ref, out_ref, adj_ref, xt0, xt1, r0, r1):
+    adj_ref[...] = list_ref[...]
     spread = spread_form()
     shape8 = (8, BLOCK)
     diff = lax.broadcasted_iota(jnp.int32, shape8, 1) - lax.broadcasted_iota(jnp.int32, shape8, 0)
@@ -244,7 +245,7 @@
             r_ref[j + half * EDGE] = adj_right(o_ref[j + half * (NBLK - EDGE)])
         return carry
 
-    lax.fori_loop(0, EDGE, build, 0, unroll=8)
+    lax.fori_loop(0, EDGE, build, 0, unroll=16)
     count = count_ref[0, 0]
     found_ref[...] = jnp.zeros_like(found_ref)
 
@@ -287,7 +288,7 @@
         out_ref[:, pl.ds(low, GCHUNK)] = attr_ref[6:7, pl.ds(low, GCHUNK)] + RATE * gain
         return carry
 
-    lax.fori_loop(0, FLOC_DEV // GCHUNK, step, 0, unroll=2)
+    lax.fori_loop(0, FLOC_DEV // GCHUNK, step, 0, unroll=16)
 
 
 VMEM = pl.BlockSpec(memory_space=pltpu.VMEM)
@@ -345,11 +346,11 @@
     owned = owned.reshape(NBLK, ATTR, BLOCK)
     up = lax.ppermute(owned[NBLK - EDGE :], "seg", [(i, i + 1) for i in range(segs - 1)])
     down = lax.ppermute(owned[:EDGE], "seg", [(i + 1, i) for i in range(segs - 1)])
-    gain = call(
+    gain, adj_list = call(
         same_kernel,
         "same_pairs",
-        shape(NBLK, BLOCK),
-        [VMEM, SMEM],
+        (shape(NBLK, BLOCK), jax.ShapeDtypeStruct((2, PADJ), jnp.int32)),
+        [VMEM, SMEM, VMEM],
         [
             pltpu.VMEM((GROUP, BLOCK, KF), BF),
             pltpu.VMEM((GROUP, BLOCK, KF), BF),
@@ -359,6 +360,7 @@
         40_000_000_000,
         owned,
         mult,
+        adj_list,
     )
     gain = call(
         adj_kernel,

time: 95.3 us -> 93.7 us (0.983)
  blocking collectives: 13.3 us -> 11.8 us
    all_to_all x1, blocking collectives: 13.3 us -> 11.8 us  [body(): lax.all_to_all(gain, 'tile', split_axis=0, concat_axis=0, tiled=True)]
where the time goes in v5:
time: 93.7 us; the launch traced here: 93.2 us
  Pallas kernels  48.5 us (52%)
  waiting for transfers between devices  16.3 us (17%)
  starting transfers between devices  14.4 us (15%)
  blocking collectives  11.8 us (13%)
  between operations  1.41 us (2%)
    pallas_call x4, Pallas kernels, call(): pl.pallas_call(kernel, out_shape=out, in_specs=ins, out_specs=jax.tree.ma...  48.5 us
    all_to_all x1, waiting for transfers between devices, body(): lax.all_to_all(send, 'tile', split_axis=0, concat_axis=0, tiled=True)  16.3 us
    all_to_all x1, blocking collectives, body(): lax.all_to_all(gain, 'tile', split_axis=0, concat_axis=0, tiled=True)  11.8 us
    all_to_all x1, starting transfers between devices, body(): lax.all_to_all(send, 'tile', split_axis=0, concat_axis=0, tiled=True)  7.77 us
    ppermute x1, starting transfers between devices, body(): lax.ppermute(owned[NBLK - EDGE:], 'seg', [(i, i + 1) for i in range(segs...  4.75 us
    ppermute x1, starting transfers between devices, body(): lax.ppermute(owned[:EDGE], 'seg', [(i + 1, i) for i in range(segs - 1)])  1.92 us
  transfers between devices with their start and end apart: 3, of which 1 were waited for; matrix products, arithmetic and copies ran while one was open for 0% of the time, Pallas kernels for 20%

profile of v5, /device:TPU:97, one launch (start us, length us, event | category | flops | bytes accessed | tf_op | source)
XLA Modules:
  0.0 93.2 jit_solution(5121784693548878882)
XLA Ops:
  0.7 22.2 %scatter.1 = (f32[256,8,128]{2,1,0:T(8,128)}, f32[8,256]{1,0:T(8,128)}, s32[2,128]{1,0:T(2,128)}) custom-call(f32[8,16384]{1,0:T(8,128)} %attr_ref.1, s32[1,16384]{1,0:T(1,128)} %bitcast.14, s32[2,1024]{1,0:T(2,128)} %bitcast.19, s32[2,128]{1,0:T(2,128)} %bitcast.20, s32[1,1]{1,0:T(1,128)S(6)} %copy.7.count_ref), custom_call_target="tpu_custom_call" | custom-call | flops 17179869184 | bytes 2097152 | tf_op jit(solution)/shard_map/scatter/pallas_call | solution.py:300
  22.9 7.8 %all-to-all-start = ((f32[32,8,8,128]{3,2,1,0:T(8,128)}), f32[32,8,8,128]{3,2,1,0:T(8,128)S(1)}, u32[]{:S(2)}, u32[]{:S(2)}) async-start(f32[32,8,8,128]{3,2,1,0:T(8,128)} %bitcast.16), calls=%async_computation | async-start | bytes 2097152 | tf_op jit(solution)/shard_map/all_to_all | solution.py:345
  31.3 16.3 %all-to-all-done = f32[32,8,8,128]{3,2,1,0:T(8,128)S(1)} async-done(((f32[32,8,8,128]{3,2,1,0:T(8,128)}), f32[32,8,8,128]{3,2,1,0:T(8,128)S(1)}, u32[]{:S(2)}, u32[]{:S(2)}) %all-to-all-start) | async-done | bytes 1048608 | tf_op jit(solution)/shard_map/all_to_all | solution.py:345
  47.6 0.0 copy-start.2
  47.6 4.8 %collective-permute-start = (f32[32,8,128]{2,1,0:T(8,128)S(1)}, f32[32,8,128]{2,1,0:T(8,128)S(1)}, u32[]{:S(2)}, u32[]{:S(2)}) collective-permute-start(f32[32,8,128]{2,1,0:T(8,128)S(1)} %bitcast.18), channel_id=1, source_target_pairs={{0,32},{32,64},{64,96},{96,128},{128,160},{160,192},{192,224},{1,3... | collective-permute-start | bytes 393224 | tf_op jit(solution)/shard_map/ppermute | solution.py:347
  52.4 1.9 %collective-permute-start.1 = (f32[32,8,128]{2,1,0:T(8,128)S(1)}, f32[32,8,128]{2,1,0:T(8,128)S(1)}, u32[]{:S(2)}, u32[]{:S(2)}) collective-permute-start(f32[32,8,128]{2,1,0:T(8,128)S(1)} %bitcast.17), channel_id=1, source_target_pairs={{32,0},{64,32},{96,64},{128,96},{160,128},{192,160},{224,192},{33,... | collective-permute-start | bytes 393224 | tf_op jit(solution)/shard_map/ppermute | solution.py:348
  54.3 0.0 copy-start.3
  54.3 0.0 copy-done.2
  54.3 0.6 copy-done.3
  55.0 18.7 %same_pairs.1 = (f32[256,128]{1,0:T(8,128)S(1)}, s32[2,128]{1,0:T(2,128)S(1)}) custom-call(f32[256,8,128]{2,1,0:T(8,128)S(1)} %bitcast.10, f32[8,256]{1,0:T(8,128)S(1)} %copy-done.2, s32[2,128]{1,0:T(2,128)S(1)} %copy-done.3), custom_call_target="tpu_custom_call" | custom-call | flops 40000000000 | bytes 2097152 | tf_op jit(solution)/shard_map/same_pairs/pallas_call | solution.py:300
  73.7 0.0 collective-permute-done.up_ref
  73.7 0.0 collective-permute-done.1.down_ref
  73.7 0.0 copy-start
  73.7 4.4 %adjacent_pairs.1 = f32[256,128]{1,0:T(8,128)S(1)} custom-call(f32[256,8,128]{2,1,0:T(8,128)S(1)} %bitcast.11, f32[32,8,128]{2,1,0:T(8,128)S(1)} %collective-permute-done.up_ref, f32[32,8,128]{2,1,0:T(8,128)S(1)} %collective-permute-done.1.down_ref, f32[256,128]{1,0:T(8,128)S(1)} %get-tuple-element.13.gain_ref, ...), custom_call_target="tpu_custom_call" | custom-call | flops 10000000000 | bytes 2097152 | tf_op jit(solution)/shard_map/adjacent_pairs/pallas_call | solution.py:300
  78.1 0.0 copy-start.1
  78.1 11.8 %all_to_all.10 = f32[32,8,128]{2,1,0:T(8,128)S(1)} all-to-all(f32[32,8,128]{2,1,0:T(8,128)S(1)} %bitcast.12), channel_id=1, replica_groups=mesh['seg'=8,'tile'=32] {'tile'}, dimensions={0} | all-to-all | bytes 262144 | tf_op jit(solution)/shard_map/all_to_all | solution.py:385
  89.9 0.0 copy-done
  89.9 0.0 copy-done.1
  89.9 3.3 %final_gather.1 = f32[1,16384]{1,0:T(1,128)} custom-call(f32[256,128]{1,0:T(8,128)S(1)} %bitcast.13, s32[1,16384]{1,0:T(1,128)S(1)} %bitcast.15, f32[8,16384]{1,0:T(8,128)S(1)} %copy-done), custom_call_target="tpu_custom_call" | custom-call | flops 10000000000 | bytes 2097152 | tf_op jit(solution)/shard_map/final_gather/pallas_call | solution.py:300
  (1 shorter events, 0.0 us)
Async XLA Ops:
  22.9 24.7 %all-to-all-start = ((f32[32,8,8,128]{3,2,1,0:T(8,128)}), f32[32,8,8,128]{3,2,1,0:T(8,128)S(1)}, u32[]{:S(2)}, u32[]{:S(2)}) async-start(f32[32,8,8,128]{3,2,1,0:T(8,128)} %bitcast.16), calls=%async_computation | async-start | bytes 2097152 | tf_op jit(solution)/shard_map/all_to_all | solution.py:345
  47.6 6.7 %copy-start.2 = (f32[8,256]{1,0:T(8,128)S(1)}, f32[8,256]{1,0:T(8,128)}, u32[]{:S(2)}) copy-start(f32[8,256]{1,0:T(8,128)} %get-tuple-element.11.mult_ref) | copy-start | bytes 24580
  47.6 26.1 %collective-permute-start = (f32[32,8,128]{2,1,0:T(8,128)S(1)}, f32[32,8,128]{2,1,0:T(8,128)S(1)}, u32[]{:S(2)}, u32[]{:S(2)}) collective-permute-start(f32[32,8,128]{2,1,0:T(8,128)S(1)} %bitcast.18), channel_id=1, source_target_pairs={{0,32},{32,64},{64,96},{96,128},{128,160},{160,192},{192,224},{1,3... | collective-permute-start | bytes 393224 | tf_op jit(solution)/shard_map/ppermute | solution.py:347
  52.4 21.3 %collective-permute-start.1 = (f32[32,8,128]{2,1,0:T(8,128)S(1)}, f32[32,8,128]{2,1,0:T(8,128)S(1)}, u32[]{:S(2)}, u32[]{:S(2)}) collective-permute-start(f32[32,8,128]{2,1,0:T(8,128)S(1)} %bitcast.17), channel_id=1, source_target_pairs={{32,0},{64,32},{96,64},{128,96},{160,128},{192,160},{224,192},{33,... | collective-permute-start | bytes 393224 | tf_op jit(solution)/shard_map/ppermute | solution.py:348
  54.3 0.7 copy-start.3
  73.7 16.2 %copy-start = (f32[8,16384]{1,0:T(8,128)S(1)}, f32[8,16384]{1,0:T(8,128)}, u32[]{:S(2)}) copy-start(f32[8,16384]{1,0:T(8,128)} %attr_ref.1) | copy-start | bytes 1572868
  78.1 11.8 %copy-start.1 = (s32[16384]{0:T(1024)S(1)}, s32[16384]{0:T(1024)}, u32[]{:S(2)}) copy-start(s32[16384]{0:T(1024)} %param.7) | copy-start | bytes 196612

commit v6 on v5

--- a/solution.py
+++ b/solution.py
@@ -49,12 +49,10 @@
 
 
 def scatter_kernel(
-    attr_hbm, slot_hbm, pairs_hbm, adj_hbm, count_ref, out_ref, mult_ref, adj_ref,
+    attr_hbm, slot_hbm, pairs_hbm, count_ref, out_ref, mult_ref,
     attr_ref, slot_ref, pairs_ref, sems, y0, y1, b0, b1, acc_ref,
 ):
-    copies = fetch(
-        (attr_hbm, slot_hbm, pairs_hbm, adj_hbm), (attr_ref, slot_ref, pairs_ref, adj_ref), sems
-    )
+    copies = fetch((attr_hbm, slot_hbm, pairs_hbm), (attr_ref, slot_ref, pairs_ref), sems)
     acc_ref[...] = jnp.zeros_like(acc_ref)
     copies[2].wait()
     first = pairs_ref[0:1, :]
@@ -100,7 +98,7 @@
         place(y1, b1)
         return carry
 
-    for n in (0, 1, 3):
+    for n in (0, 1):
         copies[n].wait()
     spread(0, y0, b0)
     lax.fori_loop(0, chunks // 2, step, 0)
@@ -318,16 +316,16 @@
     cap_blocks = NBLK // tiles
     segs = lax.axis_size("seg")
     slot_row = floc_slot.reshape(1, FLOC_DEV)
-    send, mult, adj_list = call(
+    send, mult = call(
         scatter_kernel,
         "scatter",
-        (shape(NBLK, ATTR, BLOCK), shape(8, NBLK), jax.ShapeDtypeStruct((2, PADJ), jnp.int32)),
-        [HBM, HBM, HBM, HBM, SMEM],
+        (shape(NBLK, ATTR, BLOCK), shape(8, NBLK)),
+        [HBM, HBM, HBM, SMEM],
         [
             pltpu.VMEM((ATTR, FLOC_DEV), F32),
             pltpu.VMEM((1, FLOC_DEV), jnp.int32),
             pltpu.VMEM((2, PSAME), jnp.int32),
-            pltpu.SemaphoreType.DMA((4,)),
+            pltpu.SemaphoreType.DMA((3,)),
             pltpu.VMEM((ATTR * BLOCK, 2 * CHUNK), BF),
             pltpu.VMEM((ATTR * BLOCK, 2 * CHUNK), BF),
             pltpu.VMEM((NBLK, 2 * CHUNK), BF),
@@ -338,7 +336,6 @@
         floc_attr,
         slot_row,
         same_pairs.reshape(2, PSAME),
-        adj_pairs.reshape(2, PADJ),
         same_count,
     )
     send = send.reshape(tiles, cap_blocks, ATTR, BLOCK)
@@ -360,7 +357,7 @@
         40_000_000_000,
         owned,
         mult,
-        adj_list,
+        adj_pairs.reshape(2, PADJ),
     )
     gain = call(
         adj_kernel,

time: 93.7 us -> 93.6 us (level)
  no operation moved by 1% of the time
where the time goes in v6:
time: 93.6 us; the launch traced here: 93.1 us
  Pallas kernels  48.5 us (52%)
  waiting for transfers between devices  16.3 us (17%)
  starting transfers between devices  14.4 us (15%)
  blocking collectives  11.8 us (13%)
  between operations  1.41 us (2%)
    pallas_call x4, Pallas kernels, call(): pl.pallas_call(kernel, out_shape=out, in_specs=ins, out_specs=jax.tree.ma...  48.5 us
    all_to_all x1, waiting for transfers between devices, body(): lax.all_to_all(send, 'tile', split_axis=0, concat_axis=0, tiled=True)  16.3 us
    all_to_all x1, blocking collectives, body(): lax.all_to_all(gain, 'tile', split_axis=0, concat_axis=0, tiled=True)  11.8 us
    all_to_all x1, starting transfers between devices, body(): lax.all_to_all(send, 'tile', split_axis=0, concat_axis=0, tiled=True)  7.77 us
    ppermute x1, starting transfers between devices, body(): lax.ppermute(owned[NBLK - EDGE:], 'seg', [(i, i + 1) for i in range(segs...  4.76 us
    ppermute x1, starting transfers between devices, body(): lax.ppermute(owned[:EDGE], 'seg', [(i + 1, i) for i in range(segs - 1)])  1.92 us
  transfers between devices with their start and end apart: 3, of which 1 were waited for; matrix products, arithmetic and copies ran while one was open for 0% of the time, Pallas kernels for 20%

profile of v6, /device:TPU:97, one launch (start us, length us, event | category | flops | bytes accessed | tf_op | source)
XLA Modules:
  0.0 93.1 jit_solution(13620318090425192205)
XLA Ops:
  0.7 22.2 %scatter.1 = (f32[256,8,128]{2,1,0:T(8,128)}, f32[8,256]{1,0:T(8,128)}) custom-call(f32[8,16384]{1,0:T(8,128)} %attr_ref.1, s32[1,16384]{1,0:T(1,128)} %bitcast.14, s32[2,1024]{1,0:T(2,128)} %bitcast.20, s32[1,1]{1,0:T(1,128)S(6)} %copy.7.count_ref), custom_call_target="tpu_custom_call" | custom-call | flops 17179869184 | bytes 2097152 | tf_op jit(solution)/shard_map/scatter/pallas_call | solution.py:298
  22.8 7.8 %all-to-all-start = ((f32[32,8,8,128]{3,2,1,0:T(8,128)}), f32[32,8,8,128]{3,2,1,0:T(8,128)S(1)}, u32[]{:S(2)}, u32[]{:S(2)}) async-start(f32[32,8,8,128]{3,2,1,0:T(8,128)} %bitcast.17), calls=%async_computation | async-start | bytes 2097152 | tf_op jit(solution)/shard_map/all_to_all | solution.py:342
  31.3 16.3 %all-to-all-done = f32[32,8,8,128]{3,2,1,0:T(8,128)S(1)} async-done(((f32[32,8,8,128]{3,2,1,0:T(8,128)}), f32[32,8,8,128]{3,2,1,0:T(8,128)S(1)}, u32[]{:S(2)}, u32[]{:S(2)}) %all-to-all-start) | async-done | bytes 1048608 | tf_op jit(solution)/shard_map/all_to_all | solution.py:342
  47.6 0.0 copy-start.3
  47.6 4.8 %collective-permute-start = (f32[32,8,128]{2,1,0:T(8,128)S(1)}, f32[32,8,128]{2,1,0:T(8,128)S(1)}, u32[]{:S(2)}, u32[]{:S(2)}) collective-permute-start(f32[32,8,128]{2,1,0:T(8,128)S(1)} %bitcast.19), channel_id=1, source_target_pairs={{0,32},{32,64},{64,96},{96,128},{128,160},{160,192},{192,224},{1,3... | collective-permute-start | bytes 393224 | tf_op jit(solution)/shard_map/ppermute | solution.py:344
  52.3 1.9 %collective-permute-start.1 = (f32[32,8,128]{2,1,0:T(8,128)S(1)}, f32[32,8,128]{2,1,0:T(8,128)S(1)}, u32[]{:S(2)}, u32[]{:S(2)}) collective-permute-start(f32[32,8,128]{2,1,0:T(8,128)S(1)} %bitcast.18), channel_id=1, source_target_pairs={{32,0},{64,32},{96,64},{128,96},{160,128},{192,160},{224,192},{33,... | collective-permute-start | bytes 393224 | tf_op jit(solution)/shard_map/ppermute | solution.py:345
  54.3 0.0 copy-start.2
  54.3 0.0 copy-done.3
  54.3 0.7 copy-done.2
  54.9 18.7 %same_pairs.1 = (f32[256,128]{1,0:T(8,128)S(1)}, s32[2,128]{1,0:T(2,128)S(1)}) custom-call(f32[256,8,128]{2,1,0:T(8,128)S(1)} %bitcast.10, f32[8,256]{1,0:T(8,128)S(1)} %copy-done.3, s32[2,128]{1,0:T(2,128)S(1)} %bitcast.16), custom_call_target="tpu_custom_call" | custom-call | flops 40000000000 | bytes 2097152 | tf_op jit(solution)/shard_map/same_pairs/pallas_call | solution.py:298
  73.6 0.0 collective-permute-done.up_ref
  73.6 0.0 collective-permute-done.1.down_ref
  73.6 0.0 copy-start
  73.6 4.4 %adjacent_pairs.1 = f32[256,128]{1,0:T(8,128)S(1)} custom-call(f32[256,8,128]{2,1,0:T(8,128)S(1)} %bitcast.11, f32[32,8,128]{2,1,0:T(8,128)S(1)} %collective-permute-done.up_ref, f32[32,8,128]{2,1,0:T(8,128)S(1)} %collective-permute-done.1.down_ref, f32[256,128]{1,0:T(8,128)S(1)} %get-tuple-element.11.gain_ref, ...), custom_call_target="tpu_custom_call" | custom-call | flops 10000000000 | bytes 2097152 | tf_op jit(solution)/shard_map/adjacent_pairs/pallas_call | solution.py:298
  78.0 0.0 copy-start.1
  78.0 11.8 %all_to_all.10 = f32[32,8,128]{2,1,0:T(8,128)S(1)} all-to-all(f32[32,8,128]{2,1,0:T(8,128)S(1)} %bitcast.12), channel_id=1, replica_groups=mesh['seg'=8,'tile'=32] {'tile'}, dimensions={0} | all-to-all | bytes 262144 | tf_op jit(solution)/shard_map/all_to_all | solution.py:382
  89.8 0.0 copy-done
  89.8 0.0 copy-done.1
  89.8 3.3 %final_gather.1 = f32[1,16384]{1,0:T(1,128)} custom-call(f32[256,128]{1,0:T(8,128)S(1)} %bitcast.13, s32[1,16384]{1,0:T(1,128)S(1)} %bitcast.15, f32[8,16384]{1,0:T(8,128)S(1)} %copy-done), custom_call_target="tpu_custom_call" | custom-call | flops 10000000000 | bytes 2097152 | tf_op jit(solution)/shard_map/final_gather/pallas_call | solution.py:298
  (1 shorter events, 0.0 us)
Async XLA Ops:
  22.8 24.7 %all-to-all-start = ((f32[32,8,8,128]{3,2,1,0:T(8,128)}), f32[32,8,8,128]{3,2,1,0:T(8,128)S(1)}, u32[]{:S(2)}, u32[]{:S(2)}) async-start(f32[32,8,8,128]{3,2,1,0:T(8,128)} %bitcast.17), calls=%async_computation | async-start | bytes 2097152 | tf_op jit(solution)/shard_map/all_to_all | solution.py:342
  47.6 6.7 %copy-start.3 = (f32[8,256]{1,0:T(8,128)S(1)}, f32[8,256]{1,0:T(8,128)}, u32[]{:S(2)}) copy-start(f32[8,256]{1,0:T(8,128)} %get-tuple-element.10.mult_ref) | copy-start | bytes 24580
  47.6 26.0 %collective-permute-start = (f32[32,8,128]{2,1,0:T(8,128)S(1)}, f32[32,8,128]{2,1,0:T(8,128)S(1)}, u32[]{:S(2)}, u32[]{:S(2)}) collective-permute-start(f32[32,8,128]{2,1,0:T(8,128)S(1)} %bitcast.19), channel_id=1, source_target_pairs={{0,32},{32,64},{64,96},{96,128},{128,160},{160,192},{192,224},{1,3... | collective-permute-start | bytes 393224 | tf_op jit(solution)/shard_map/ppermute | solution.py:344
  52.3 21.3 %collective-permute-start.1 = (f32[32,8,128]{2,1,0:T(8,128)S(1)}, f32[32,8,128]{2,1,0:T(8,128)S(1)}, u32[]{:S(2)}, u32[]{:S(2)}) collective-permute-start(f32[32,8,128]{2,1,0:T(8,128)S(1)} %bitcast.18), channel_id=1, source_target_pairs={{32,0},{64,32},{96,64},{128,96},{160,128},{192,160},{224,192},{33,... | collective-permute-start | bytes 393224 | tf_op jit(solution)/shard_map/ppermute | solution.py:345
  54.3 0.7 copy-start.2
  73.6 16.2 %copy-start = (f32[8,16384]{1,0:T(8,128)S(1)}, f32[8,16384]{1,0:T(8,128)}, u32[]{:S(2)}) copy-start(f32[8,16384]{1,0:T(8,128)} %attr_ref.1) | copy-start | bytes 1572868
  78.0 11.8 %copy-start.1 = (s32[16384]{0:T(1024)S(1)}, s32[16384]{0:T(1024)}, u32[]{:S(2)}) copy-start(s32[16384]{0:T(1024)} %param.7) | copy-start | bytes 196612
